TPU v7x, 512 devices: a whole 4x8x8 slice. The times are simulated.
512 devices in a mesh: owner: 32 (over z, x_hi, core), resp: 16 (over x_lo, y).
Axes of the slice: x: 4 (x_hi: 2, x_lo: 2; x = x_hi * 2 + x_lo), y: 8, z: 8, core: 2. Of those that a mesh axis runs over, the one named last changes fastest.
Arguments:
- queries: bfloat16 [32, 16, 128, 2560], P('owner', 'resp'), may hold values from -8 to 8
- resp_keys: bfloat16 [32, 16, 128, 512], P('owner', 'resp'), may hold values from -8 to 8
- resp_values: bfloat16 [32, 16, 128, 512], P('owner', 'resp'), may hold values from -6 to 6
- out_grad: bfloat16 [32, 16, 128, 2560], P('owner', 'resp'), may hold values from -6 to 6
- prefix_keys: bfloat16 [32, 256, 512], P('owner', 'resp'), may hold values from -6 to 6
- prefix_values: bfloat16 [32, 256, 512], P('owner', 'resp'), may hold values from -6 to 6
- device_prompt: int32 [32, 16], P('owner', 'resp'), may hold values from 0 to 31, as said below
- resp_len: int32 [32, 16], P('owner', 'resp'), may hold values from 32 to 128, as said below
Outputs:
- dquery: bfloat16 [32, 16, 128, 2560], P('owner', 'resp')
- dresp_keys: bfloat16 [32, 16, 128, 512], P('owner', 'resp')
- dresp_values: bfloat16 [32, 16, 128, 512], P('owner', 'resp')
- dprefix_keys: float32 [32, 256, 512], P('owner', 'resp')
- dprefix_values: float32 [32, 256, 512], P('owner', 'resp')
Inputs may be any that keep to these rules, and one draw needn't show every extreme that they name: `device_prompt`: A device's prompt is its owner index plus -1, 0 or 1. On every owner index but the first, the device at resp index 0 holds the prompt below; on every owner index but the last, the device at resp index 15 holds the prompt above. `resp_len`: some device holds a response of 128 tokens.
All inputs are finite; a program needn't handle non-finite values.
Results may differ from a plain program's by a relative error of at most 0.0082.
Values may be sent and summed in bfloat16 or wider, within the bound.
A program may use at most 64 MiB of HBM per device.

v0:
```python
import math

import jax
import jax.numpy as jnp
from jax import lax
from jax.sharding import PartitionSpec as P

HQ = 20
HK = 4
DH = 128


def padded(block, sides, width):
    for axis, dim in sides:
        count = lax.axis_size(axis)
        forward = [(i, i + 1) for i in range(count - 1)]
        backward = [(target, source) for source, target in forward]
        low = lax.ppermute(
            lax.slice_in_dim(block, block.shape[dim] - width, None, axis=dim), axis, forward
        )
        high = lax.ppermute(lax.slice_in_dim(block, 0, width, axis=dim), axis, backward)
        block = jnp.concatenate([low, block, high], axis=dim)
    return block


def head_grads(query_head, key_head, value_head, grad_head, visible):
    score_scale = 1.0 / math.sqrt(DH)
    scores = (
        jnp.einsum("rgd,kd->grk", query_head, key_head, preferred_element_type=jnp.float32)
        * score_scale
    )
    scores = jnp.where(visible[None], scores, jnp.float32(-1e30))
    row_top = jnp.max(scores, -1, keepdims=True)
    exp_terms = jnp.exp(scores - row_top)
    probs = exp_terms / jnp.sum(exp_terms, -1, keepdims=True)
    probs_low = probs.astype(jnp.bfloat16)
    output = jnp.einsum("grk,kd->rgd", probs_low, value_head, preferred_element_type=jnp.float32)
    delta = jnp.sum(grad_head.astype(jnp.float32) * output, -1)
    dprobs = jnp.einsum("rgd,kd->grk", grad_head, value_head, preferred_element_type=jnp.float32)
    dscores = (probs * (dprobs - jnp.transpose(delta)[:, :, None])).astype(jnp.bfloat16)
    dquery = (
        jnp.einsum("grk,kd->rgd", dscores, key_head, preferred_element_type=jnp.float32)
        * score_scale
    )
    dkeys = (
        jnp.einsum("grk,rgd->kd", dscores, query_head, preferred_element_type=jnp.float32)
        * score_scale
    )
    dvalues = jnp.einsum("grk,rgd->kd", probs_low, grad_head, preferred_element_type=jnp.float32)
    return (dquery, dkeys, dvalues)


def body(
    queries, resp_keys, resp_values, out_grad, prefix_keys, prefix_values, device_prompt, resp_len
):
    prompt_offset = device_prompt[0, 0] - lax.axis_index("owner")
    stacked = jnp.stack((prefix_keys, prefix_values), axis=1)
    whole_prefix = lax.all_gather(stacked, "resp", axis=2, tiled=True)
    near_prefix = padded(whole_prefix, (("owner", 0),), 1)
    chosen = lax.dynamic_index_in_dim(near_prefix, prompt_offset + 1, 0, keepdims=False)
    prefix_len = chosen.shape[1]
    slot_count = queries.shape[2]
    resp_length = resp_len[0, 0]
    row_index = jnp.arange(slot_count, dtype=jnp.int32)
    key_slots = jnp.arange(prefix_len + slot_count, dtype=jnp.int32) - prefix_len
    visible = (key_slots[None, :] < 0) | (key_slots[None, :] <= row_index[:, None]) & (
        key_slots[None, :] < resp_length
    )
    valid_rows = (row_index < resp_length).astype(jnp.bfloat16)
    group_size = HQ // HK
    keys_all = jnp.concatenate([chosen[0], resp_keys[0, 0]], 0).reshape(
        prefix_len + slot_count, HK, DH
    )
    values_all = jnp.concatenate([chosen[1], resp_values[0, 0]], 0).reshape(
        prefix_len + slot_count, HK, DH
    )
    query_all = queries[0, 0].reshape(slot_count, HK, group_size, DH)
    grad_all = (out_grad[0, 0] * valid_rows[:, None]).reshape(slot_count, HK, group_size, DH)
    query_parts = []
    key_parts = []
    value_parts = []
    for head_index in range(HK):
        dquery_head, dkeys_head, dvalues_head = head_grads(
            query_all[:, head_index],
            keys_all[:, head_index],
            values_all[:, head_index],
            grad_all[:, head_index],
            visible,
        )
        query_parts.append(dquery_head)
        key_parts.append(dkeys_head)
        value_parts.append(dvalues_head)
    dquery = jnp.stack(query_parts, 1).reshape(slot_count, HQ * DH).astype(jnp.bfloat16)
    dkeys = jnp.stack(key_parts, 1).reshape(prefix_len + slot_count, HK * DH)
    dvalues = jnp.stack(value_parts, 1).reshape(prefix_len + slot_count, HK * DH)
    prefix_grads = jnp.stack((dkeys[:prefix_len], dvalues[:prefix_len]))
    slot_pick = (jnp.arange(3, dtype=jnp.int32) == prompt_offset + 1).astype(jnp.float32)
    placed = slot_pick[:, None, None, None] * prefix_grads[None]
    summed = lax.psum_scatter(placed, "resp", scatter_dimension=2, tiled=True)
    rim_sums = padded(summed, (("owner", 0),), 1)
    owned = summed[1] + rim_sums[0] + rim_sums[4]
    return (
        dquery[None, None],
        dkeys[prefix_len:].astype(jnp.bfloat16)[None, None],
        dvalues[prefix_len:].astype(jnp.bfloat16)[None, None],
        owned[0][None],
        owned[1][None],
    )


def solution(mesh):
    return jax.shard_map(
        body,
        mesh=mesh,
        in_specs=(
            P("owner", "resp", None, None),
            P("owner", "resp", None, None),
            P("owner", "resp", None, None),
            P("owner", "resp", None, None),
            P("owner", "resp", None),
            P("owner", "resp", None),
            P("owner", "resp"),
            P("owner", "resp"),
        ),
        out_specs=(
            P("owner", "resp", None, None),
            P("owner", "resp", None, None),
            P("owner", "resp", None, None),
            P("owner", "resp", None),
            P("owner", "resp", None),
        ),
        check_vma=False,
    )
```

profile of v0, /device:TPU:1, one launch (start us, length us, event | category | flops | bytes accessed | tf_op | source)
XLA Modules:
  0.0 187.7 jit_solution(15767900069106389141)
XLA Ops:
  7.2 0.8 pad_maximum_fusion.6
  8.1 30.3 %all_gather.3 = bf16[1,2,256,512]{3,1,0,2:T(2,128)(2,1)S(1)} all-gather(bf16[1,2,16,512]{3,1,0,2:T(2,128)(2,1)S(1)} %copy.108), channel_id=1, replica_groups=mesh['owner'=32,'resp'=16] {'resp'}, dimensions={2}, use_global_device_ids=true | all-gather | bytes 557056 | tf_op jit(solution)/shard_map/all_gather | solution.py:58
  38.4 1.2 copy.109
  39.6 10.9 %collective-permute-start.1 = (bf16[1,2,256,512]{2,3,1,0:T(8,128)(2,1)}, bf16[1,2,256,512]{2,3,1,0:T(8,128)(2,1)}, u32[]{:S(2)}, u32[]{:S(2)}) collective-permute-start(bf16[1,2,256,512]{2,3,1,0:T(8,128)(2,1)} %copy.109), channel_id=1, source_target_pairs={{16,0},{32,16},{48,32},{64,48},{80,64},{96,80},{112,96},{128,112},... | collective-permute-start | bytes 1572872 | tf_op jit(solution)/shard_map/ppermute | solution.py:21
  50.5 3.2 %collective-permute-start = (bf16[1,2,256,512]{2,3,1,0:T(8,128)(2,1)}, bf16[1,2,256,512]{2,3,1,0:T(8,128)(2,1)}, u32[]{:S(2)}, u32[]{:S(2)}) collective-permute-start(bf16[1,2,256,512]{2,3,1,0:T(8,128)(2,1)} %copy.109), channel_id=1, source_target_pairs={{0,16},{16,32},{32,48},{48,64},{64,80},{80,96},{96,112},{112,128},... | collective-permute-start | bytes 1572872 | tf_op jit(solution)/shard_map/ppermute | solution.py:18
  55.1 1.0 copy.112
  56.1 0.1 copy.114
  56.2 1.0 copy.117
  57.3 0.1 copy.119
  57.4 0.3 copy.115
  57.7 0.3 copy.120
  58.1 0.3 copy.121
  58.4 0.2 fusion.63
  58.6 0.1 broadcast_multiply_fusion.1
  58.8 0.2 collective-permute-done.1
  58.9 4.5 %collective-permute-done = bf16[1,2,256,512]{2,3,1,0:T(8,128)(2,1)} collective-permute-done((bf16[1,2,256,512]{2,3,1,0:T(8,128)(2,1)}, bf16[1,2,256,512]{2,3,1,0:T(8,128)(2,1)}, u32[]{:S(2)}, u32[]{:S(2)}) %collective-permute-start) | collective-permute-done | bytes 524320 | tf_op jit(solution)/shard_map/ppermute | solution.py:18
  63.5 1.3 fusion.57
  64.9 0.2 copy.118
  65.0 0.2 copy.113
  65.2 0.7 fusion.76
  65.9 0.5 fusion.114
  66.5 0.5 fusion.50
  66.9 0.3 convolution_bitcast_fusion.9
  67.2 1.4 fusion.117
  68.7 1.3 fusion.59
  69.9 0.5 fusion.49
  70.4 1.0 convolution_bitcast_fusion.10
  71.4 0.5 fusion.120
  71.9 0.1 fusion.58
  72.0 0.5 fusion.48
  72.5 1.0 convolution_bitcast_fusion.11
  73.5 0.3 fusion.30
  73.8 1.0 fusion.43
  74.8 0.3 fusion.29
  75.1 1.0 fusion.45
  76.1 0.3 fusion.28
  76.4 0.8 copy-done.5
  77.2 1.0 fusion.47
  78.2 1.4 fusion.113
  79.6 1.3 fusion.61
  80.9 0.3 convolution_bitcast_fusion.8
  81.2 0.5 fusion.51
  81.7 1.6 fusion.31
  83.3 0.3 fusion.41
  83.9 0.2 copy-done.7
  84.1 0.6 copy-done
  84.8 0.3 copy.161
  85.2 2.2 %broadcast_multiply_fusion = f32[3,2,256,512]{3,2,1,0:T(8,128)} fusion(f32[2,256,512]{2,1,0:T(8,128)S(1)} %copy.161, f32[3]{0:T(128)S(1)} %compare_convert_fusion), kind=kLoop, calls=%fused_computation.7 | loop fusion | flops 786432 | bytes 4194316 | tf_op jit(solution)/shard_map/mul | solution.py:98
  87.4 1.1 slice.294
  88.5 0.3 fusion.53
  88.8 0.3 fusion.54
  89.1 0.3 fusion.55
  89.4 0.3 fusion.52
  89.7 66.8 %reduce-scatter.2.cloned.1.call-done = f32[3,2,16,512]{3,2,1,0:T(8,128)} async-done(((f32[3,2,256,512]{3,2,1,0:T(8,128)}), f32[3,2,16,512]{3,2,1,0:T(8,128)}) %reduce-scatter.2.cloned.1.call-update) | async-done | bytes 196624 | tf_op jit(solution)/shard_map/reduce_scatter | solution.py:99
  156.6 0.9 fusion.112
  157.5 14.8 %collective-permute-start.2 = (f32[1,2,16,512]{3,2,1,0:T(8,128)S(1)}, f32[1,2,16,512]{3,2,1,0:T(8,128)S(1)}, u32[]{:S(2)}, u32[]{:S(2)}) collective-permute-start(f32[1,2,16,512]{3,2,1,0:T(8,128)S(1)} %get-tuple-element.22), channel_id=1, source_target_pairs={{0,16},{16,32},{32,48},{48,64},{64,80},{80,96},{96,112},{112,128},... | collective-permute-start | bytes 196616 | tf_op jit(solution)/shard_map/ppermute | solution.py:18
  172.3 1.9 %collective-permute-start.3 = (f32[1,2,16,512]{3,2,1,0:T(8,128)S(1)}, f32[1,2,16,512]{3,2,1,0:T(8,128)S(1)}, u32[]{:S(2)}, u32[]{:S(2)}) collective-permute-start(f32[1,2,16,512]{3,2,1,0:T(8,128)S(1)} %get-tuple-element.23), channel_id=1, source_target_pairs={{16,0},{32,16},{48,32},{64,48},{80,64},{96,80},{112,96},{128,112},... | collective-permute-start | bytes 196616 | tf_op jit(solution)/shard_map/ppermute | solution.py:21
  174.2 0.1 pad_maximum_fusion.3
  174.3 1.1 copy.162
  175.4 0.8 copy.163
  176.2 0.8 copy.164
  176.9 2.4 %collective-permute-done.3 = f32[1,2,16,512]{3,2,1,0:T(8,128)S(1)} collective-permute-done((f32[1,2,16,512]{3,2,1,0:T(8,128)S(1)}, f32[1,2,16,512]{3,2,1,0:T(8,128)S(1)}, u32[]{:S(2)}, u32[]{:S(2)}) %collective-permute-start.3) | collective-permute-done | bytes 65568 | tf_op jit(solution)/shard_map/ppermute | solution.py:21
  179.4 0.9 fusion.78
  180.2 0.6 slice_bitcast_fusion.32
  (62 shorter events, 0.6 us)
Async XLA Ops:
  7.2 50.2 %copy-start.19 = (bf16[1,1,128,2560]{3,2,1,0:T(8,128)(2,1)S(1)}, bf16[1,1,128,2560]{3,2,1,0:T(8,128)(2,1)}, u32[]{:S(2)}) copy-start(bf16[1,1,128,2560]{3,2,1,0:T(8,128)(2,1)} %param.8) | copy-start | bytes 1966084
  7.2 50.6 %copy-start.20 = (bf16[1,1,128,2560]{3,2,1,0:T(8,128)(2,1)S(1)}, bf16[1,1,128,2560]{3,2,1,0:T(8,128)(2,1)}, u32[]{:S(2)}) copy-start(bf16[1,1,128,2560]{3,2,1,0:T(8,128)(2,1)} %param.11) | copy-start | bytes 1966084
  7.2 149.4 %reduce-scatter.2.cloned.1.call-start = ((), (), s32[]{:S(2)}) async-start(), calls=%async_computation.1 | async-start | bytes 3342336 | tf_op jit(solution)/shard_map/reduce_scatter | solution.py:99
  39.6 19.3 %collective-permute-start.1 = (bf16[1,2,256,512]{2,3,1,0:T(8,128)(2,1)}, bf16[1,2,256,512]{2,3,1,0:T(8,128)(2,1)}, u32[]{:S(2)}, u32[]{:S(2)}) collective-permute-start(bf16[1,2,256,512]{2,3,1,0:T(8,128)(2,1)} %copy.109), channel_id=1, source_target_pairs={{16,0},{32,16},{48,32},{64,48},{80,64},{96,80},{112,96},{128,112},... | collective-permute-start | bytes 1572872 | tf_op jit(solution)/shard_map/ppermute | solution.py:21
  50.5 12.9 %collective-permute-start = (bf16[1,2,256,512]{2,3,1,0:T(8,128)(2,1)}, bf16[1,2,256,512]{2,3,1,0:T(8,128)(2,1)}, u32[]{:S(2)}, u32[]{:S(2)}) collective-permute-start(bf16[1,2,256,512]{2,3,1,0:T(8,128)(2,1)} %copy.109), channel_id=1, source_target_pairs={{0,16},{16,32},{32,48},{48,64},{64,80},{80,96},{96,112},{112,128},... | collective-permute-start | bytes 1572872 | tf_op jit(solution)/shard_map/ppermute | solution.py:18
  65.2 13.0 %copy-start.21 = (bf16[384,128,1]{1,0,2:T(8,128)(2,1)}, bf16[384,128,1]{1,0,2:T(8,128)(2,1)S(1)}, u32[]{:S(2)}) copy-start(bf16[384,128,1]{1,0,2:T(8,128)(2,1)S(1)} %fusion.77) | copy-start | bytes 294916
  66.4 3.6 %copy-start.9 = (f32[5,128,384]{1,2,0:T(8,128)}, f32[5,128,384]{1,2,0:T(8,128)S(1)}, u32[]{:S(2)}) copy-start(f32[5,128,384]{1,2,0:T(8,128)S(1)} %get-tuple-element.29) | copy-start | bytes 2949124
  71.9 1.6 copy-start.12
  71.9 1.6 copy-start.10
  72.5 2.4 %copy-start.11 = (f32[5,128,384]{1,2,0:T(8,128)S(1)}, f32[5,128,384]{1,2,0:T(8,128)}, u32[]{:S(2)}) copy-start(f32[5,128,384]{1,2,0:T(8,128)} %get-tuple-element.31) | copy-start | bytes 2949124
  73.8 2.6 %copy-start.1 = (bf16[5,128,384]{1,2,0:T(8,128)(2,1)}, bf16[5,128,384]{1,2,0:T(8,128)(2,1)S(1)}, u32[]{:S(2)}) copy-start(bf16[5,128,384]{1,2,0:T(8,128)(2,1)S(1)} %fusion.30) | copy-start | bytes 1474564
  73.8 2.3 %copy-start.13 = (f32[5,128,384]{1,2,0:T(8,128)S(1)}, f32[5,128,384]{1,2,0:T(8,128)}, u32[]{:S(2)}) copy-start(f32[5,128,384]{1,2,0:T(8,128)} %copy-done.12) | copy-start | bytes 2949124
  75.1 4.4 %copy-start.3 = (bf16[5,128,384]{1,2,0:T(8,128)(2,1)}, bf16[5,128,384]{1,2,0:T(8,128)(2,1)S(1)}, u32[]{:S(2)}) copy-start(bf16[5,128,384]{1,2,0:T(8,128)(2,1)S(1)} %fusion.29) | copy-start | bytes 1474564
  76.4 0.8 copy-start.5
  78.2 3.0 %copy-start.23 = (bf16[384,128,1]{1,0,2:T(8,128)(2,1)S(1)}, bf16[384,128,1]{1,0,2:T(8,128)(2,1)}, u32[]{:S(2)}) copy-start(bf16[384,128,1]{1,0,2:T(8,128)(2,1)} %fusion.76) | copy-start | bytes 294916
  80.9 2.8 %copy-start.16 = (f32[384,1,128]{0,2,1:T(8,128)S(1)}, f32[384,1,128]{0,2,1:T(8,128)}, u32[]{:S(2)}) copy-start(f32[384,1,128]{0,2,1:T(8,128)} %fusion.43) | copy-start | bytes 589828
  80.9 2.8 %copy-start.17 = (f32[384,1,128]{0,2,1:T(8,128)S(1)}, f32[384,1,128]{0,2,1:T(8,128)}, u32[]{:S(2)}) copy-start(f32[384,1,128]{0,2,1:T(8,128)} %fusion.45) | copy-start | bytes 589828
  80.9 2.8 %copy-start.18 = (f32[384,1,128]{0,2,1:T(8,128)S(1)}, f32[384,1,128]{0,2,1:T(8,128)}, u32[]{:S(2)}) copy-start(f32[384,1,128]{0,2,1:T(8,128)} %fusion.47) | copy-start | bytes 589828
  81.7 2.1 %copy-start.14 = (f32[384,1,128]{0,2,1:T(8,128)S(1)}, f32[384,1,128]{0,2,1:T(8,128)}, u32[]{:S(2)}) copy-start(f32[384,1,128]{0,2,1:T(8,128)} %convolution_bitcast_fusion.10) | copy-start | bytes 589828
  81.7 2.1 %copy-start.15 = (f32[384,1,128]{0,2,1:T(8,128)S(1)}, f32[384,1,128]{0,2,1:T(8,128)}, u32[]{:S(2)}) copy-start(f32[384,1,128]{0,2,1:T(8,128)} %convolution_bitcast_fusion.11) | copy-start | bytes 589828
  83.3 0.8 copy-start.7
  83.9 0.9 copy-start
  85.1 3.4 %copy-start.2 = (bf16[5,128,384]{1,2,0:T(8,128)(2,1)S(1)}, bf16[5,128,384]{1,2,0:T(8,128)(2,1)}, u32[]{:S(2)}) copy-start(bf16[5,128,384]{1,2,0:T(8,128)(2,1)} %copy-done.1) | copy-start | bytes 1474564
  87.4 1.5 copy-start.4
  87.4 1.8 copy-start.6
  87.4 2.1 %copy-start.8 = (bf16[5,128,384]{1,2,0:T(8,128)(2,1)S(1)}, bf16[5,128,384]{1,2,0:T(8,128)(2,1)}, u32[]{:S(2)}) copy-start(bf16[5,128,384]{1,2,0:T(8,128)(2,1)} %copy-done.7) | copy-start | bytes 1474564
  87.4 2.1 %copy-start.22 = (bf16[384,128,1]{1,0,2:T(8,128)(2,1)S(1)}, bf16[384,128,1]{1,0,2:T(8,128)(2,1)}, u32[]{:S(2)}) copy-start(bf16[384,128,1]{1,0,2:T(8,128)(2,1)} %copy-done.21) | copy-start | bytes 294916
  157.5 19.5 %collective-permute-start.2 = (f32[1,2,16,512]{3,2,1,0:T(8,128)S(1)}, f32[1,2,16,512]{3,2,1,0:T(8,128)S(1)}, u32[]{:S(2)}, u32[]{:S(2)}) collective-permute-start(f32[1,2,16,512]{3,2,1,0:T(8,128)S(1)} %get-tuple-element.22), channel_id=1, source_target_pairs={{0,16},{16,32},{32,48},{48,64},{64,80},{80,96},{96,112},{112,128},... | collective-permute-start | bytes 196616 | tf_op jit(solution)/shard_map/ppermute | solution.py:18
  172.3 7.1 %collective-permute-start.3 = (f32[1,2,16,512]{3,2,1,0:T(8,128)S(1)}, f32[1,2,16,512]{3,2,1,0:T(8,128)S(1)}, u32[]{:S(2)}, u32[]{:S(2)}) collective-permute-start(f32[1,2,16,512]{3,2,1,0:T(8,128)S(1)} %get-tuple-element.23), channel_id=1, source_target_pairs={{16,0},{32,16},{48,32},{64,48},{80,64},{96,80},{112,96},{128,112},... | collective-permute-start | bytes 196616 | tf_op jit(solution)/shard_map/ppermute | solution.py:21
Sparse Core Ops, SparseCore 0:
  87.5 69.0 reduce-scatter.1
where the time goes:
time: 188 us
  waiting for transfers between devices  74 us (39%)
  starting transfers between devices  30.8 us (16%)
  blocking collectives  30.3 us (16%)
  between operations  16 us (9%)
  matrix products  15.1 us (8%)
  local copies, waits for them, and re-layouts  12.3 us (7%)
  other arithmetic  9.29 us (5%)
    reduce_scatter x1, waiting for transfers between devices, body(): summed = lax.psum_scatter(placed, 'resp', scatter_dimension=2, tiled=True)  66.8 us
    all_gather x1, blocking collectives, body(): whole_prefix = lax.all_gather(stacked, 'resp', axis=2, tiled=True)  30.3 us
    ppermute x2, starting transfers between devices, padded(): lax.ppermute(lax.slice_in_dim(block, block.shape[dim] - width, None, axis...  18 us
    ppermute x2, starting transfers between devices, padded(): lax.ppermute(lax.slice_in_dim(block, 0, width, axis=dim), axis, backward)  12.8 us
    unnamed x55, local copies, waits for them, and re-layouts  7 us
    ppermute x2, waiting for transfers between devices, padded(): lax.ppermute(lax.slice_in_dim(block, block.shape[dim] - width, None, axis...  4.54 us
  transfers between devices with their start and end apart: 5, of which 4 were waited for; matrix products, arithmetic and copies ran while one was open for 5% of the time, Pallas kernels for 0%

commit v1 on v0

v1 whole, which is shorter than its diff:
```python
import functools
import math

import jax
import jax.numpy as jnp
from jax import lax
from jax.experimental import pallas as pl
from jax.experimental.pallas import tpu as pltpu
from jax.sharding import PartitionSpec as P

HQ = 20
HK = 4
DH = 128
GROUP = HQ // HK
MESH = pl.DeviceIdType.MESH
F32 = jnp.float32
BF16 = jnp.bfloat16


def dot(a, b, dims):
    return lax.dot_general(a, b, (dims, ((), ())), preferred_element_type=F32)


def slot_weights(tile):
    offset = tile.astype(F32)
    return [jnp.maximum(1.0 - jnp.abs(offset - s), 0.0) for s in (-1.0, 0.0, 1.0)]


def kernel(
    n_owner, n_resp, rows, prefix_len, slots,
    prompt_ref, len_ref, q_hbm, g_hbm, rk_hbm, rv_hbm, pk_hbm, pv_hbm,
    dq_hbm, drk_hbm, drv_hbm, dpk_hbm, dpv_hbm,
    q_all, g_all, kv_all, near, my_tile, tiles, stage, grad_out, grad_in,
    acc, rim_out, rim_in, dq_all, dr_all, dp_all,
    load_sem, near_load_sem, store_sem, near_send, near_recv, tile_send, tile_recv,
    gather_send, gather_recv, grad_send, grad_recv, rim_send, rim_recv,
):
    o = lax.axis_index("owner")
    r = lax.axis_index("resp")
    above = lax.rem(o + 1, n_owner)
    below = lax.rem(o + n_owner - 1, n_owner)
    mine = pl.ds(pl.multiple_of(r * rows, rows), rows)

    def peer(d):
        return lax.rem(r + d, n_resp)

    near_loads = []
    for h in range(HK):
        for kv, ref in enumerate((pk_hbm, pv_hbm)):
            near_loads.append(
                pltpu.make_async_copy(
                    ref.at[:, pl.ds(h * DH, DH)], near.at[1, h, kv], near_load_sem.at[h, kv]
                )
            )
    loads = []
    for h in range(HK):
        for kv, ref in enumerate((rk_hbm, rv_hbm)):
            loads.append(
                pltpu.make_async_copy(
                    ref.at[:, pl.ds(h * DH, DH)],
                    kv_all.at[h, kv, pl.ds(prefix_len, slots)],
                    load_sem.at[len(loads)],
                )
            )
        for g in range(GROUP):
            for ref, target in ((q_hbm, q_all), (g_hbm, g_all)):
                loads.append(
                    pltpu.make_async_copy(
                        ref.at[:, pl.ds((h * GROUP + g) * DH, DH)],
                        target.at[h, pl.ds(g * slots, slots)],
                        load_sem.at[len(loads)],
                    )
                )
    for copy in near_loads:
        copy.start()
    barrier = pltpu.get_barrier_semaphore()
    for target in (above, below):
        pl.semaphore_signal(barrier, inc=1, device_id=(target, r), device_id_type=MESH)

    def greet(d, carry):
        pl.semaphore_signal(barrier, inc=1, device_id=(o, peer(d)), device_id_type=MESH)
        return carry

    lax.fori_loop(1, n_resp, greet, 0)
    for copy in loads:
        copy.start()
    my_tile[...] = jnp.full((rows, DH), (prompt_ref[0, 0] - o).astype(F32)).astype(BF16)
    tiles[r] = my_tile[...]
    for copy in near_loads:
        copy.wait()
    pl.semaphore_wait(barrier, n_resp + 1)

    def near_copy(side):
        return pltpu.make_async_remote_copy(
            src_ref=near.at[1],
            dst_ref=near.at[2 * side],
            send_sem=near_send.at[side],
            recv_sem=near_recv.at[side],
            device_id=((above, below)[side], r),
            device_id_type=MESH,
        )

    def tile_copy(d):
        return pltpu.make_async_remote_copy(
            src_ref=my_tile,
            dst_ref=tiles.at[r],
            send_sem=tile_send.at[d],
            recv_sem=tile_recv.at[d],
            device_id=(o, peer(d)),
            device_id_type=MESH,
        )

    def gather_copy(h, d):
        return pltpu.make_async_remote_copy(
            src_ref=stage.at[h, d],
            dst_ref=kv_all.at[h, :, mine],
            send_sem=gather_send.at[h, d],
            recv_sem=gather_recv.at[h, d],
            device_id=(o, peer(d)),
            device_id_type=MESH,
        )

    def grad_copy(h, d):
        return pltpu.make_async_remote_copy(
            src_ref=grad_out.at[h, peer(d)],
            dst_ref=grad_in.at[h, r],
            send_sem=grad_send.at[h, d],
            recv_sem=grad_recv.at[h, d],
            device_id=(o, peer(d)),
            device_id_type=MESH,
        )

    def rim_copy(h, side):
        return pltpu.make_async_remote_copy(
            src_ref=rim_out.at[h, side],
            dst_ref=rim_in.at[h, side],
            send_sem=rim_send.at[h, side],
            recv_sem=rim_recv.at[h, side],
            device_id=((below, above)[side], r),
            device_id_type=MESH,
        )

    for side in range(2):
        near_copy(side).start()

    def each_peer(action):
        def step(d, carry):
            action(d)
            return carry

        lax.fori_loop(1, n_resp, step, 0)

    each_peer(lambda d: tile_copy(d).start())
    for side in range(2):
        near_copy(side).wait_recv()
    each_peer(lambda d: tile_copy(d).wait_recv())

    def pick(h, tile):
        weights = [w.astype(BF16) for w in slot_weights(tile)]
        return sum(weights[s] * near[s, h] for s in range(3))

    for h in range(HK):

        def send_part(d, h=h):
            stage[h, d] = pick(h, tiles[peer(d)])
            gather_copy(h, d).start()

        each_peer(send_part)
        kv_all[h, :, mine, :] = pick(h, my_tile[...])

    for copy in loads:
        copy.wait()

    length = len_ref[0, 0]
    key_index = lax.broadcasted_iota(jnp.int32, (slots, slots), 0)
    row_index = lax.broadcasted_iota(jnp.int32, (slots, slots), 1)
    hidden = jnp.where((key_index <= row_index) & (key_index < length), 0.0, -1e30)
    hidden = jnp.concatenate([hidden] * GROUP, axis=1)
    valid = jnp.where(key_index < length, 1.0, 0.0).astype(BF16)
    valid = jnp.concatenate([valid] * GROUP, axis=0)
    scale = 1.0 / math.sqrt(DH)
    exp_scale = scale * math.log2(math.e)

    def head(h, carry):
        each_peer(lambda d: gather_copy(h, d).wait_recv())
        keys = kv_all[h, 0]
        values = kv_all[h, 1]
        queries = q_all[h]
        grads = g_all[h] * valid
        scores = dot(keys, queries, ((1,), (1,)))
        scores = jnp.concatenate([scores[:prefix_len], scores[prefix_len:] + hidden], axis=0)
        top = jnp.max(scores, axis=0, keepdims=True)
        terms = jnp.exp2((scores - top) * exp_scale)
        probs = terms * (1.0 / jnp.sum(terms, axis=0, keepdims=True))
        probs_low = probs.astype(BF16)
        dprobs = dot(values, grads, ((1,), (1,)))
        delta = jnp.sum(probs * dprobs, axis=0, keepdims=True)
        dscores = (probs * (dprobs - delta)).astype(BF16)
        dkeys = dot(dscores, queries, ((1,), (0,))) * scale
        dvalues = dot(probs_low, grads, ((1,), (0,)))
        keys_t = keys.astype(F32).T.astype(BF16)
        dquery_t = dot(keys_t, dscores, ((1,), (0,))) * scale
        for kv, value in enumerate((dkeys, dvalues)):
            grad_out[h, :, kv] = value[:prefix_len].astype(BF16).reshape(n_resp, rows, DH)
            dr_all[h, kv] = value[prefix_len:].astype(BF16)
        each_peer(lambda d: grad_copy(h, d).start())
        dq_all[h] = dquery_t.T.astype(BF16)
        grad_in[h, r] = grad_out[h, r]
        return carry

    lax.fori_loop(0, HK, head, 0)

    stores = []
    for h in range(HK):
        for kv, ref in enumerate((drk_hbm, drv_hbm)):
            stores.append(
                pltpu.make_async_copy(
                    dr_all.at[h, kv], ref.at[:, pl.ds(h * DH, DH)], store_sem.at[len(stores)]
                )
            )
        for g in range(GROUP):
            stores.append(
                pltpu.make_async_copy(
                    dq_all.at[h, pl.ds(g * slots, slots)],
                    dq_hbm.at[:, pl.ds((h * GROUP + g) * DH, DH)],
                    store_sem.at[len(stores)],
                )
            )
    for copy in stores:
        copy.start()

    def collect(h, carry):
        each_peer(lambda d: grad_copy(h, d).wait_recv())

        def add(p, sums):
            weights = slot_weights(tiles[p])
            term = grad_in[h, p].astype(F32)
            return tuple(sums[s] + weights[s] * term for s in range(3))

        zero = jnp.zeros((2, rows, DH), F32)
        sums = lax.fori_loop(0, n_resp, add, (zero, zero, zero))
        rim_out[h, 0] = sums[0].astype(BF16)
        rim_out[h, 1] = sums[2].astype(BF16)
        acc[h] = sums[1]
        for side in range(2):
            rim_copy(h, side).start()
        return carry

    lax.fori_loop(0, HK, collect, 0)
    for h in range(HK):
        for side in range(2):
            rim_copy(h, side).wait_recv()
        total = acc[h] + rim_in[h, 0].astype(F32) + rim_in[h, 1].astype(F32)
        dp_all[0, :, pl.ds(h * DH, DH)] = total[0]
        dp_all[1, :, pl.ds(h * DH, DH)] = total[1]
    for kv, ref in enumerate((dpk_hbm, dpv_hbm)):
        copy = pltpu.make_async_copy(dp_all.at[kv], ref, store_sem.at[len(stores)])
        copy.start()
        stores.append(copy)
    for side in range(2):
        near_copy(side).wait_send()
    each_peer(lambda d: tile_copy(d).wait_send())

    def drain(h, carry):
        each_peer(lambda d: gather_copy(h, d).wait_send())
        each_peer(lambda d: grad_copy(h, d).wait_send())
        for side in range(2):
            rim_copy(h, side).wait_send()
        return carry

    lax.fori_loop(0, HK, drain, 0)
    for copy in stores:
        copy.wait()


def body(n_owner, n_resp, queries, resp_keys, resp_values, out_grad, prefix_keys, prefix_values, device_prompt, resp_len):
    slots = queries.shape[2]
    rows = prefix_keys.shape[1]
    prefix_len = rows * n_resp
    total = prefix_len + slots
    anywhere = pl.BlockSpec(memory_space=pl.ANY)
    scalar = pl.BlockSpec(memory_space=pltpu.SMEM)
    dma = pltpu.SemaphoreType.DMA
    vmem = pltpu.VMEM
    flops = 2 * 5 * HQ * slots * total * DH
    outs = pl.pallas_call(
        functools.partial(kernel, n_owner, n_resp, rows, prefix_len, slots),
        out_shape=(
            jax.ShapeDtypeStruct((slots, HQ * DH), BF16),
            jax.ShapeDtypeStruct((slots, HK * DH), BF16),
            jax.ShapeDtypeStruct((slots, HK * DH), BF16),
            jax.ShapeDtypeStruct((rows, HK * DH), F32),
            jax.ShapeDtypeStruct((rows, HK * DH), F32),
        ),
        in_specs=[scalar] * 2 + [anywhere] * 6,
        out_specs=(anywhere,) * 5,
        scratch_shapes=[
            vmem((HK, GROUP * slots, DH), BF16),
            vmem((HK, GROUP * slots, DH), BF16),
            vmem((HK, 2, total, DH), BF16),
            vmem((3, HK, 2, rows, DH), BF16),
            vmem((rows, DH), BF16),
            vmem((n_resp, rows, DH), BF16),
            vmem((HK, n_resp, 2, rows, DH), BF16),
            vmem((HK, n_resp, 2, rows, DH), BF16),
            vmem((HK, n_resp, 2, rows, DH), BF16),
            vmem((HK, 2, rows, DH), F32),
            vmem((HK, 2, 2, rows, DH), BF16),
            vmem((HK, 2, 2, rows, DH), BF16),
            vmem((HK, GROUP * slots, DH), BF16),
            vmem((HK, 2, slots, DH), BF16),
            vmem((2, rows, HK * DH), F32),
            dma((HK * 2 + HQ * 2,)),
            dma((HK, 2)),
            dma((HK * 2 + HQ + 2,)),
            dma((2,)),
            dma((2,)),
            dma((n_resp,)),
            dma((n_resp,)),
            dma((HK, n_resp)),
            dma((HK, n_resp)),
            dma((HK, n_resp)),
            dma((HK, n_resp)),
            dma((HK, 2)),
            dma((HK, 2)),
        ],
        compiler_params=pltpu.CompilerParams(
            collective_id=0, has_side_effects=True, vmem_limit_bytes=40 * 2**20
        ),
        cost_estimate=pl.CostEstimate(flops=flops, bytes_accessed=4 * 2**20, transcendentals=HQ * slots * total),
    )(
        device_prompt, resp_len, queries[0, 0], out_grad[0, 0], resp_keys[0, 0], resp_values[0, 0],
        prefix_keys[0], prefix_values[0],
    )
    dquery, dkeys, dvalues, dprefix_keys, dprefix_values = outs
    return dquery[None, None], dkeys[None, None], dvalues[None, None], dprefix_keys[None], dprefix_values[None]


def solution(mesh):
    row = P("owner", "resp", None, None)
    return jax.shard_map(
        functools.partial(body, mesh.shape["owner"], mesh.shape["resp"]),
        mesh=mesh,
        in_specs=(row, row, row, row, P("owner", "resp", None), P("owner", "resp", None), P("owner", "resp"), P("owner", "resp")),
        out_specs=(row, row, row, P("owner", "resp", None), P("owner", "resp", None)),
        check_vma=False,
    )
```

time: 188 us -> 62.6 us (0.33)
  the two profiles are of different devices: /device:TPU:1 before, /device:TPU:8 now
where the time goes in v1:
time: 62.6 us; the launch traced here: 62.2 us
  Pallas kernels  51.5 us (82%)
  local copies, waits for them, and re-layouts  8.79 us (14%)
  between operations  1.95 us (3%)
    pallas_call x1, Pallas kernels, body(): pl.pallas_call(functools.partial(kernel, n_owner, n_resp, rows, prefix_le...  51.5 us
    unnamed x17, local copies, waits for them, and re-layouts  8.79 us

profile of v1, /device:TPU:8, one launch (start us, length us, event | category | flops | bytes accessed | tf_op | source)
XLA Modules:
  0.0 62.2 jit_solution(9820513203554664452)
XLA Ops:
  1.9 0.0 copy-start
  1.9 1.1 %copy-done = bf16[1,1,128,2560]{3,2,1,0:T(8,128)(2,1)S(1)} copy-done((bf16[1,1,128,2560]{3,2,1,0:T(8,128)(2,1)S(1)}, bf16[1,1,128,2560]{3,2,1,0:T(8,128)(2,1)}, u32[]{:S(2)}) %copy-start) | copy-done | bytes 655384
  3.0 0.0 copy-start.1
  3.0 1.1 %copy-done.1 = bf16[1,1,128,2560]{3,2,1,0:T(8,128)(2,1)S(1)} copy-done((bf16[1,1,128,2560]{3,2,1,0:T(8,128)(2,1)S(1)}, bf16[1,1,128,2560]{3,2,1,0:T(8,128)(2,1)}, u32[]{:S(2)}) %copy-start.1) | copy-done | bytes 655384
  4.1 0.0 copy-start.2
  4.1 0.9 %copy-done.2 = bf16[1,1,128,512]{3,2,1,0:T(8,128)(2,1)S(1)} copy-done((bf16[1,1,128,512]{3,2,1,0:T(8,128)(2,1)S(1)}, bf16[1,1,128,512]{3,2,1,0:T(8,128)(2,1)}, u32[]{:S(2)}) %copy-start.2) | copy-done | bytes 131096
  5.0 0.0 copy-start.3
  5.0 0.9 %copy-done.3 = bf16[1,1,128,512]{3,2,1,0:T(8,128)(2,1)S(1)} copy-done((bf16[1,1,128,512]{3,2,1,0:T(8,128)(2,1)S(1)}, bf16[1,1,128,512]{3,2,1,0:T(8,128)(2,1)}, u32[]{:S(2)}) %copy-start.3) | copy-done | bytes 131096
  5.9 0.0 copy-start.4
  5.9 0.7 %copy-done.4 = bf16[1,16,512]{2,1,0:T(8,128)(2,1)S(1)} copy-done((bf16[1,16,512]{2,1,0:T(8,128)(2,1)S(1)}, bf16[1,16,512]{2,1,0:T(8,128)(2,1)}, u32[]{:S(2)}) %copy-start.4) | copy-done | bytes 16408
  6.6 0.0 copy-start.5
  6.6 0.7 %copy-done.5 = bf16[1,16,512]{2,1,0:T(8,128)(2,1)S(1)} copy-done((bf16[1,16,512]{2,1,0:T(8,128)(2,1)S(1)}, bf16[1,16,512]{2,1,0:T(8,128)(2,1)}, u32[]{:S(2)}) %copy-start.5) | copy-done | bytes 16408
  7.3 51.5 %shard_map.119 = (bf16[128,2560]{1,0:T(8,128)(2,1)S(1)}, bf16[128,512]{1,0:T(8,128)(2,1)S(1)}, bf16[128,512]{1,0:T(8,128)(2,1)S(1)}, f32[16,512]{1,0:T(8,128)S(1)}, f32[16,512]{1,0:T(8,128)S(1)}) custom-call(s32[1,1]{1,0:T(1,128)S(6)} %copy.18.prompt_ref, s32[1,1]{1,0:T(1,128)S(6)} %copy.19.len_ref, bf16[128,2560]{1,0:T(8,128)(2,1)S(1)} %bitcast.16, ...), custom_call_target="tpu_custom_call" | custom-call | flops 1258291200 | bytes 4194304 | tf_op jit(solution)/shard_map/pallas_call | solution.py:286
  58.9 0.8 %copy.20 = bf16[1,1,128,2560]{3,2,1,0:T(8,128)(2,1)} copy(bf16[1,1,128,2560]{3,2,1,0:T(8,128)(2,1)S(1)} %bitcast.11) | data formatting | bytes 1310720
  59.7 0.7 %copy.21 = bf16[1,1,128,512]{3,2,1,0:T(8,128)(2,1)} copy(bf16[1,1,128,512]{3,2,1,0:T(8,128)(2,1)S(1)} %bitcast.13) | data formatting | bytes 262144
  60.3 0.7 %copy.22 = bf16[1,1,128,512]{3,2,1,0:T(8,128)(2,1)} copy(bf16[1,1,128,512]{3,2,1,0:T(8,128)(2,1)S(1)} %bitcast.12) | data formatting | bytes 262144
  61.0 0.6 copy.23
  61.6 0.6 copy.24
Async XLA Ops:
  1.9 1.1 %copy-start = (bf16[1,1,128,2560]{3,2,1,0:T(8,128)(2,1)S(1)}, bf16[1,1,128,2560]{3,2,1,0:T(8,128)(2,1)}, u32[]{:S(2)}) copy-start(bf16[1,1,128,2560]{3,2,1,0:T(8,128)(2,1)} %param.8) | copy-start | bytes 1966084
  3.0 1.1 %copy-start.1 = (bf16[1,1,128,2560]{3,2,1,0:T(8,128)(2,1)S(1)}, bf16[1,1,128,2560]{3,2,1,0:T(8,128)(2,1)}, u32[]{:S(2)}) copy-start(bf16[1,1,128,2560]{3,2,1,0:T(8,128)(2,1)} %param.11) | copy-start | bytes 1966084
  4.1 0.9 %copy-start.2 = (bf16[1,1,128,512]{3,2,1,0:T(8,128)(2,1)S(1)}, bf16[1,1,128,512]{3,2,1,0:T(8,128)(2,1)}, u32[]{:S(2)}) copy-start(bf16[1,1,128,512]{3,2,1,0:T(8,128)(2,1)} %param.9) | copy-start | bytes 393220
  5.0 0.9 %copy-start.3 = (bf16[1,1,128,512]{3,2,1,0:T(8,128)(2,1)S(1)}, bf16[1,1,128,512]{3,2,1,0:T(8,128)(2,1)}, u32[]{:S(2)}) copy-start(bf16[1,1,128,512]{3,2,1,0:T(8,128)(2,1)} %param.10) | copy-start | bytes 393220
  5.9 0.7 %copy-start.4 = (bf16[1,16,512]{2,1,0:T(8,128)(2,1)S(1)}, bf16[1,16,512]{2,1,0:T(8,128)(2,1)}, u32[]{:S(2)}) copy-start(bf16[1,16,512]{2,1,0:T(8,128)(2,1)} %param.12) | copy-start | bytes 49156
  6.6 0.7 %copy-start.5 = (bf16[1,16,512]{2,1,0:T(8,128)(2,1)S(1)}, bf16[1,16,512]{2,1,0:T(8,128)(2,1)}, u32[]{:S(2)}) copy-start(bf16[1,16,512]{2,1,0:T(8,128)(2,1)} %param.13) | copy-start | bytes 49156

commit v2 on v1

--- a/solution.py
+++ b/solution.py
@@ -270,6 +270,18 @@
 
     lax.fori_loop(0, HK, drain, 0)
     for copy in stores:
+        copy.wait()
+
+
+def publish(*refs):
+    count = len(refs) // 2
+    sems = refs[-1]
+    copies = [
+        pltpu.make_async_copy(refs[i], refs[count + i], sems.at[i]) for i in range(count)
+    ]
+    for copy in copies:
+        copy.start()
+    for copy in copies:
         copy.wait()
 
 
@@ -325,14 +337,21 @@
             dma((HK, 2)),
         ],
         compiler_params=pltpu.CompilerParams(
-            collective_id=0, has_side_effects=True, vmem_limit_bytes=40 * 2**20
+            collective_id=0, has_side_effects=True, vmem_limit_bytes=63 * 2**20
         ),
         cost_estimate=pl.CostEstimate(flops=flops, bytes_accessed=4 * 2**20, transcendentals=HQ * slots * total),
     )(
         device_prompt, resp_len, queries[0, 0], out_grad[0, 0], resp_keys[0, 0], resp_values[0, 0],
         prefix_keys[0], prefix_values[0],
     )
-    dquery, dkeys, dvalues, dprefix_keys, dprefix_values = outs
+    dquery, dkeys, dvalues, dprefix_keys, dprefix_values = pl.pallas_call(
+        publish,
+        out_shape=[jax.ShapeDtypeStruct(x.shape, x.dtype) for x in outs],
+        in_specs=[anywhere] * len(outs),
+        out_specs=[anywhere] * len(outs),
+        scratch_shapes=[dma((len(outs),))],
+        compiler_params=pltpu.CompilerParams(vmem_limit_bytes=63 * 2**20),
+    )(*outs)
     return dquery[None, None], dkeys[None, None], dvalues[None, None], dprefix_keys[None], dprefix_values[None]
 
 

time: 62.6 us -> 84.5 us (1.35)
  Pallas kernels: 51.5 us -> 82.4 us
  local copies, waits for them, and re-layouts: 8.79 us -> 0 us
    pallas_call x0 -> x1, Pallas kernels: none -> 30.9 us  [body(): pl.pallas_call(publish, out_shape=[jax.ShapeDtypeStruct(x.shape, x.dtype)...]
    unnamed x17 -> x0, local copies, waits for them, and re-layouts: 8.79 us -> none
where the time goes in v2:
time: 84.5 us; the launch traced here: 84.3 us
  Pallas kernels  82.4 us (98%)
  between operations  1.93 us (2%)
    pallas_call x1, Pallas kernels, body(): pl.pallas_call(functools.partial(kernel, n_owner, n_resp, rows, prefix_le...  51.4 us
    pallas_call x1, Pallas kernels, body(): pl.pallas_call(publish, out_shape=[jax.ShapeDtypeStruct(x.shape, x.dtype)...  30.9 us

profile of v2, /device:TPU:8, one launch (start us, length us, event | category | flops | bytes accessed | tf_op | source)
XLA Modules:
  0.0 84.3 jit_solution(5780476702427081694)
XLA Ops:
  1.9 51.4 %shard_map.119 = (bf16[128,2560]{1,0:T(8,128)(2,1)}, bf16[128,512]{1,0:T(8,128)(2,1)}, bf16[128,512]{1,0:T(8,128)(2,1)}, f32[16,512]{1,0:T(8,128)}, f32[16,512]{1,0:T(8,128)}) custom-call(s32[1,1]{1,0:T(1,128)S(6)} %copy.13.prompt_ref, s32[1,1]{1,0:T(1,128)S(6)} %copy.14.len_ref, bf16[128,2560]{1,0:T(8,128)(2,1)} %bitcast.11, bf16[128,2560]{1,0:T(8,128)(2,1)} %bitcast.12, ...), custom_call_target="tpu_custom_call" | custom-call | flops 1258291200 | bytes 4194304 | tf_op jit(solution)/shard_map/pallas_call | solution.py:298
  53.4 30.9 %shard_map.120 = (bf16[128,2560]{1,0:T(8,128)(2,1)}, bf16[128,512]{1,0:T(8,128)(2,1)}, bf16[128,512]{1,0:T(8,128)(2,1)}, f32[16,512]{1,0:T(8,128)}, f32[16,512]{1,0:T(8,128)}) custom-call(bf16[128,2560]{1,0:T(8,128)(2,1)} %get-tuple-element.15.refs_0_, bf16[128,512]{1,0:T(8,128)(2,1)} %get-tuple-element.16.refs_1_, ...), custom_call_target="tpu_custom_call" | custom-call | tf_op jit(solution)/shard_map/pallas_call | solution.py:347

commit v3 on v0

v3 whole, which is shorter than its diff:
```python
import functools
import math

import jax
import jax.numpy as jnp
from jax import lax
from jax.experimental import pallas as pl
from jax.experimental.pallas import tpu as pltpu
from jax.sharding import PartitionSpec as P

HQ = 20
HK = 4
DH = 128
GROUP = HQ // HK
MESH = pl.DeviceIdType.MESH
F32 = jnp.float32
BF16 = jnp.bfloat16


def dot(a, b, dims):
    return lax.dot_general(a, b, (dims, ((), ())), preferred_element_type=F32)


SLOTS = 4
NY = 8
STEPS = (-1, 3, 1, -3, 4, 0, -2, 2)
KINDS = ((0, 2, 1), (2, 2, -1), (4, 1, None), (5, 3, 0))
PARTS = 2
PER_PART = HK // PARTS


def slot_weights(tile):
    return [jnp.maximum(1.0 - jnp.abs(tile - s), 0.0) for s in range(SLOTS)]


def kernel(
    n_owner, rows, prefix_len, slots,
    prompt_ref, len_ref, q_hbm, g_hbm, rk_hbm, rv_hbm, pk_hbm, pv_hbm,
    dq_hbm, drk_hbm, drv_hbm, dpk_hbm, dpv_hbm,
    q_all, g_all, resp_all, near, tiles, stage, kv_all, grad_out, grad_in,
    sums_out, sums_in, dq_all, dr_all, dp_all,
    load_sem, own_sem, store_sem, near_send, near_recv, tile_send, tile_recv,
    gather_send, gather_recv, grad_send, grad_recv, sums_send, sums_recv,
):
    o = lax.axis_index("owner")
    r = lax.axis_index("resp")
    pairs = n_owner // 2
    k = o // 2
    c = lax.rem(o, 2)
    xl = r // NY
    y = lax.rem(r, NY)
    me = 2 * c + xl
    prompts = (pk_hbm, pv_hbm)
    has_below = k > 0
    has_above = k < pairs - 1
    side = 2 * c - 1
    next_in = (k + side >= 0) & (k + side < pairs)
    other_in = (k - side >= 0) & (k - side < pairs)
    pair_next = lax.rem(k + side + pairs, pairs)
    pair_other = lax.rem(k - side + pairs, pairs)
    pair_below = lax.rem(k + pairs - 1, pairs)
    pair_above = lax.rem(k + 1, pairs)

    y_of = {step: lax.rem(y + (step + NY), NY) for step in (-2, -1, 0, 1, 2)}

    def device(core, x, step):
        return (2 * k + core, x * NY + y_of[step])

    def column(owner, step):
        return (owner, xl * NY + y_of[step])

    def remote(src, dst, send, recv, target):
        return pltpu.make_async_remote_copy(
            src_ref=src, dst_ref=dst, send_sem=send, recv_sem=recv, device_id=target, device_id_type=MESH
        )

    def away(spot):
        return me != spot

    barrier = pltpu.get_barrier_semaphore()

    def signal(target):
        pl.semaphore_signal(barrier, inc=1, device_id=target, device_id_type=MESH)

    for step in (2, -2, 0, 1, -1):
        for spot in range(4):
            if step == 0:
                pl.when(away(spot))(lambda spot=spot: signal(device(spot // 2, spot % 2, 0)))
            else:
                signal(device(spot // 2, spot % 2, step))

    @pl.when(next_in)
    def _():
        for step in (2, -2, 0):
            for kv in range(2):
                signal(column(2 * pair_next + kv, step))

    @pl.when(other_in)
    def _():
        for step in (2, -2, 0):
            signal(column(2 * pair_other + c, step))

    tiles[0, me] = jnp.full((1, DH), (prompt_ref[0, 0] - (2 * k - 1)).astype(F32))

    @pl.when(k == 0)
    def _():
        for where in range(3):
            near[where, 0] = jnp.zeros_like(near[where, 0])

    @pl.when(k == pairs - 1)
    def _():
        for where in range(3):
            near[where, 3] = jnp.zeros_like(near[where, 3])

    @pl.when(jnp.logical_not(next_in))
    def _():
        for where in range(3):
            for kv in range(2):
                sums_in[where, 1, kv] = jnp.zeros_like(sums_in[where, 1, kv])

    own_copies = [pltpu.make_async_copy(prompts[kv], near.at[0, 1 + c], own_sem.at[0]) for kv in range(2)]
    for kv in range(2):
        pl.when(c == kv)(own_copies[kv].start)

    pl.semaphore_wait(barrier, 19 + 6 * next_in.astype(jnp.int32) + 3 * other_in.astype(jnp.int32))

    near_copies = []
    for where, step in ((1, 2), (2, -2), (0, 0)):
        for kind, (pair, slot) in enumerate(((k, 1 + c), (pair_next, 3 - 3 * c))):
            for kv in range(2):
                copy = remote(
                    prompts[kv], near.at[where, slot], near_send.at[where, kind, kv], near_recv.at[where, slot],
                    column(2 * pair + kv, step),
                )
                condition = next_in if kind == 1 else (c != kv if where == 0 else None)
                near_copies.append((condition, copy))

    def tile_copy(spot, step, kind):
        return remote(
            tiles.at[0, me], tiles.at[kind, me], tile_send.at[kind, spot], tile_recv.at[kind, me],
            device(spot // 2, spot % 2, step),
        )

    tile_copies = []
    for kind, step in ((1, -1), (2, 1), (0, 0)):
        for spot in range(4):
            tile_copies.append((away(spot) if kind == 0 else None, tile_copy(spot, step, kind)))
    for core, step in ((0, -2), (1, 2)):
        for spot in range(4):
            tile_copies.append((c == core, tile_copy(spot, step, 3)))

    def each(copies, action):
        for condition, copy in copies:
            if condition is None:
                getattr(copy, action)()
            else:
                pl.when(condition)(getattr(copy, action))

    each(near_copies, "start")
    each(tile_copies, "start")

    loads = [
        pltpu.make_async_copy(rk_hbm, resp_all.at[0], load_sem.at[0]),
        pltpu.make_async_copy(rv_hbm, resp_all.at[1], load_sem.at[1]),
        pltpu.make_async_copy(q_hbm, q_all, load_sem.at[2]),
        pltpu.make_async_copy(g_hbm, g_all, load_sem.at[3]),
    ]

    def arrived(ref, sem):
        remote(ref, ref, near_send.at[0, 0, 0], sem, device(0, 0, 1)).wait_recv()

    for kind in (1, 2, 0, 3):
        for spot in range(4):
            wait = functools.partial(arrived, tiles.at[kind, spot], tile_recv.at[kind, spot])
            if kind == 0:
                pl.when(away(spot))(wait)
            else:
                wait()
    for where in (1, 2, 0):
        for slot in range(SLOTS):
            wait = functools.partial(arrived, near.at[where, slot], near_recv.at[where, slot])
            if slot == 0:
                pl.when(has_below)(wait)
            elif slot == 3:
                pl.when(has_above)(wait)
            elif where == 0:
                pl.when(c != slot - 1)(wait)
            else:
                wait()
    for kv in range(2):
        pl.when(c == kv)(own_copies[kv].wait)

    weights = [[slot_weights(tiles[kind, spot]) for spot in range(4)] for kind in range(4)]

    def gather_copy(part, spot, kind, step):
        first, count, _ = KINDS[kind]
        heads = pl.ds(part * PER_PART, PER_PART)
        blocks = pl.ds(first, count)
        return remote(
            stage.at[heads, spot, blocks], kv_all.at[heads, c, xl, blocks],
            gather_send.at[part, spot, kind], gather_recv.at[part, me, kind], device(spot // 2, spot % 2, step),
        )

    kept = ((1, 2), (2, 1), None, (0, 1, 2))
    gather_copies = []
    for part in range(PARTS):
        block = {}
        for kind, step in ((0, -1), (1, 1), (2, None), (3, 0)):
            first = KINDS[kind][0]
            source = (1, 2, 3, 0)[kind]
            for spot in range(4):
                low = [jnp.broadcast_to(w, (rows, DH)).astype(BF16) for w in weights[{0: 2, 1: 1, 2: 3, 3: 0}[kind]][spot]]
                for j, where in enumerate(kept[kind] or ((1,) if spot < 2 else (2,))):
                    for h in range(part * PER_PART, (part + 1) * PER_PART):
                        columns = slice(h * DH, (h + 1) * DH)
                        stage[h, spot, first + j] = sum(low[s] * near[where, s, :, columns] for s in range(SLOTS))
                copy = gather_copy(part, spot, kind, step if kind != 2 else (2 if spot < 2 else -2))
                condition = away(spot) if kind == 3 else None
                each([(condition, copy)], "start")
                gather_copies.append((condition, copy))
        for h in range(part * PER_PART, (part + 1) * PER_PART):
            kv_all[h, c, xl, 5:8] = stage[h, me, 5:8]
        if part == 0:
            for copy in loads:
                copy.start()

    def gather_arrived(part):
        heads = pl.ds(part * PER_PART, PER_PART)
        for kind, (first, count, _) in enumerate(KINDS):
            for spot in range(4):
                wait = functools.partial(
                    arrived, kv_all.at[heads, spot // 2, spot % 2, pl.ds(first, count)], gather_recv.at[part, spot, kind]
                )
                if kind == 3:
                    pl.when(away(spot))(wait)
                else:
                    wait()

    length = len_ref[0, 0]
    key_index = lax.broadcasted_iota(jnp.int32, (slots, slots), 0)
    row_index = lax.broadcasted_iota(jnp.int32, (slots, slots), 1)
    hidden = jnp.where((key_index <= row_index) & (key_index < length), 0.0, -1e30)
    hidden = jnp.concatenate([hidden] * GROUP, axis=1)
    valid = jnp.where(key_index < length, 1.0, 0.0).astype(BF16)
    scale = 1.0 / math.sqrt(DH)
    exp_scale = scale * math.log2(math.e)

    for copy in loads:
        copy.wait()

    def grad_copies(h):
        copies = []
        for kind, (first, count, step) in enumerate(KINDS):
            blocks = pl.ds(first, count)
            for spot in range(4):
                def make(step, spot=spot, kind=kind, blocks=blocks):
                    return remote(
                        grad_out.at[h, spot // 2, spot % 2, blocks], grad_in.at[h, me, blocks],
                        grad_send.at[h, spot, kind], grad_recv.at[h, me, kind], device(spot // 2, spot % 2, step),
                    )
                if kind == 2:
                    copies.append((c == 0, make(-2)))
                    copies.append((c == 1, make(2)))
                else:
                    copies.append((away(spot) if kind == 3 else None, make(step)))
        return copies

    def sums_copies(first, count):
        heads = pl.ds(first, count)
        part = 0 if first == 0 else 1
        copies = []
        for where, step in ((1, -2), (2, 2), (0, 0)):
            for slot, owner, condition in (
                (0, 2 * pair_below + 1, has_below), (3, 2 * pair_above, has_above), (1, 2 * k, None), (2, 2 * k + 1, None),
            ):
                kind = 1 if slot in (0, 3) else 0
                if where == 0 and kind == 0:
                    condition = c != slot - 1
                copies.append((condition, remote(
                    sums_out.at[where, slot, heads], sums_in.at[where, kind, c, heads],
                    sums_send.at[part, where, slot], sums_recv.at[part, where, kind, c], column(owner, step),
                )))
        return copies

    def combine(h):
        for kind, (first, count, _) in enumerate(KINDS):
            for spot in range(4):
                wait = functools.partial(arrived, grad_in.at[h, spot, pl.ds(first, count)], grad_recv.at[h, spot, kind])
                if kind == 3:
                    pl.when(away(spot))(wait)
                else:
                    wait()
        grad_in[h, me, 5:8] = grad_out[h, c, xl, 5:8]
        below = [(6, 0, s) for s in range(4)] + [(0, 2, s) for s in range(4)] + [(3, 1, s) for s in range(4)] + [(4, 3, 0), (4, 3, 1)]
        above = [(7, 0, s) for s in range(4)] + [(1, 2, s) for s in range(4)] + [(2, 1, s) for s in range(4)] + [(4, 3, 2), (4, 3, 3)]
        here = [(5, 0, s) for s in range(4)]
        for where, terms in enumerate((here, below, above)):
            totals = [None] * SLOTS
            for block, kind, spot in terms:
                piece = grad_in[h, spot, block].astype(F32)
                for s in range(SLOTS):
                    term = weights[kind][spot][s] * piece
                    totals[s] = term if totals[s] is None else totals[s] + term
            for s in range(SLOTS):
                sums_out[where, s, h] = totals[s].astype(BF16)

    def attend(h):
        def columns(ref, first, count=1):
            return ref[:, pl.ds(pl.multiple_of(first, DH), count * DH)]

        keys = jnp.concatenate([kv_all[h, 0].reshape(prefix_len, DH), columns(resp_all.at[0], h * DH)], axis=0)
        values = jnp.concatenate([kv_all[h, 1].reshape(prefix_len, DH), columns(resp_all.at[1], h * DH)], axis=0)
        queries = jnp.concatenate([columns(q_all, (h * GROUP + g) * DH) for g in range(GROUP)], axis=0)
        grads = jnp.concatenate([columns(g_all, (h * GROUP + g) * DH) * valid for g in range(GROUP)], axis=0)
        scores = dot(keys, queries, ((1,), (1,)))
        scores = jnp.concatenate([scores[:prefix_len], scores[prefix_len:] + hidden], axis=0)
        top = jnp.max(scores, axis=0, keepdims=True)
        terms = jnp.exp2((scores - top) * exp_scale)
        probs = terms * (1.0 / jnp.sum(terms, axis=0, keepdims=True))
        probs_low = probs.astype(BF16)
        dprobs = dot(values, grads, ((1,), (1,)))
        delta = jnp.sum(probs * dprobs, axis=0, keepdims=True)
        dscores = (probs * (dprobs - delta)).astype(BF16)
        dkeys = dot(dscores, queries, ((1,), (0,))) * scale
        dvalues = dot(probs_low, grads, ((1,), (0,)))
        for kv, value in enumerate((dkeys, dvalues)):
            grad_out[h, kv] = value[:prefix_len].astype(BF16).reshape(2, NY, rows, DH)
            dr_all[kv, :, pl.ds(pl.multiple_of(h * DH, DH), DH)] = value[prefix_len:].astype(BF16)
        each(grad_copies(h), "start")
        keys_t = keys.astype(F32).T.astype(BF16)
        dquery_t = dot(keys_t, dscores, ((1,), (0,))) * scale
        for g in range(GROUP):
            dquery = dquery_t[:, g * slots:(g + 1) * slots].T.astype(BF16)
            dq_all[:, pl.ds(pl.multiple_of((h * GROUP + g) * DH, DH), DH)] = dquery

    def dq_store(h):
        columns = pl.ds(pl.multiple_of(h * GROUP * DH, DH), GROUP * DH)
        return pltpu.make_async_copy(dq_all.at[:, columns], dq_hbm.at[:, columns], store_sem.at[4 + h])

    def head(h, carry):
        for part in range(PARTS):
            pl.when(h == part * PER_PART)(functools.partial(gather_arrived, part))
        attend(h)
        dq_store(h).start()
        pl.when(h >= 1)(lambda: combine(h - 1))
        return carry

    lax.fori_loop(0, HK, head, 0)
    early = sums_copies(0, HK - 1)
    late = sums_copies(HK - 1, 1)
    each(early, "start")
    stores = [
        pltpu.make_async_copy(dr_all.at[0], drk_hbm, store_sem.at[0]),
        pltpu.make_async_copy(dr_all.at[1], drv_hbm, store_sem.at[1]),
    ]
    for copy in stores:
        copy.start()
    combine(HK - 1)
    each(late, "start")
    sums_in[0, 0, c] = sums_out[0, 1 + c]
    each(near_copies, "wait_send")
    each(tile_copies, "wait_send")
    each(gather_copies, "wait_send")

    for part, heads in enumerate((pl.ds(0, HK - 1), pl.ds(HK - 1, 1))):
        for where in (0, 1, 2):
            for kind in range(2):
                for kv in range(2):
                    wait = functools.partial(
                        arrived, sums_in.at[where, kind, kv, heads], sums_recv.at[part, where, kind, kv]
                    )
                    if kind == 1:
                        pl.when(next_in)(wait)
                    elif where == 0:
                        pl.when(c != kv)(wait)
                    else:
                        wait()
    for kv in range(2):
        for h in range(HK):
            total = jnp.zeros((rows, DH), F32)
            for where in (0, 1, 2):
                for kind in range(2):
                    total += sums_in[where, kind, kv, h].astype(F32)
            dp_all[kv, :, h * DH:(h + 1) * DH] = total
    for kv, ref in enumerate((dpk_hbm, dpv_hbm)):
        copy = pltpu.make_async_copy(dp_all.at[kv], ref, store_sem.at[2 + kv])
        copy.start()
        stores.append(copy)

    each(early, "wait_send")
    each(late, "wait_send")

    def drain(h, carry):
        each(grad_copies(h), "wait_send")
        dq_store(h).wait()
        return carry

    lax.fori_loop(0, HK, drain, 0)
    for copy in stores:
        copy.wait()


def publish(*refs):
    count = (len(refs) - 2) // 3
    ins, outs, held = refs[:count], refs[count:2 * count], refs[2 * count:3 * count]
    in_sem, out_sem = refs[-2:]
    loads = [pltpu.make_async_copy(ins[i], held[i], in_sem.at[i]) for i in range(count)]
    stores = [pltpu.make_async_copy(held[i], outs[i], out_sem.at[i]) for i in range(count)]
    for copy in loads:
        copy.start()
    for i in range(count):
        loads[i].wait()
        stores[i].start()
    for copy in stores:
        copy.wait()


def body(n_owner, n_resp, queries, resp_keys, resp_values, out_grad, prefix_keys, prefix_values, device_prompt, resp_len):
    slots = queries.shape[2]
    rows = prefix_keys.shape[1]
    prefix_len = rows * n_resp
    total = prefix_len + slots
    anywhere = pl.BlockSpec(memory_space=pl.ANY)
    scalar = pl.BlockSpec(memory_space=pltpu.SMEM)
    dma = pltpu.SemaphoreType.DMA
    vmem = pltpu.VMEM
    width = HK * DH
    flops = 2 * 5 * HQ * slots * total * DH
    outs = pl.pallas_call(
        functools.partial(kernel, n_owner, rows, prefix_len, slots),
        out_shape=(
            jax.ShapeDtypeStruct((slots, HQ * DH), BF16),
            jax.ShapeDtypeStruct((slots, width), BF16),
            jax.ShapeDtypeStruct((slots, width), BF16),
            jax.ShapeDtypeStruct((rows, width), F32),
            jax.ShapeDtypeStruct((rows, width), F32),
        ),
        in_specs=[scalar] * 2 + [anywhere] * 6,
        out_specs=(anywhere,) * 5,
        scratch_shapes=[
            vmem((slots, HQ * DH), BF16),
            vmem((slots, HQ * DH), BF16),
            vmem((2, slots, width), BF16),
            vmem((3, SLOTS, rows, width), BF16),
            vmem((4, 4, 1, DH), F32),
            vmem((HK, 4, NY, rows, DH), BF16),
            vmem((HK, 2, 2, NY, rows, DH), BF16),
            vmem((HK, 2, 2, NY, rows, DH), BF16),
            vmem((HK, 4, NY, rows, DH), BF16),
            vmem((3, SLOTS, HK, rows, DH), BF16),
            vmem((3, 2, 2, HK, rows, DH), BF16),
            vmem((slots, HQ * DH), BF16),
            vmem((2, slots, width), BF16),
            vmem((2, rows, width), F32),
            dma((4,)),
            dma((1,)),
            dma((4 + HK,)),
            dma((3, 2, 2)),
            dma((3, SLOTS)),
            dma((4, 4)),
            dma((4, 4)),
            dma((PARTS, 4, 4)),
            dma((PARTS, 4, 4)),
            dma((HK, 4, 4)),
            dma((HK, 4, 4)),
            dma((2, 3, SLOTS)),
            dma((2, 3, 2, 2)),
        ],
        compiler_params=pltpu.CompilerParams(
            collective_id=0, has_side_effects=True, vmem_limit_bytes=63 * 2**20
        ),
        cost_estimate=pl.CostEstimate(flops=flops, bytes_accessed=4 * 2**20, transcendentals=HQ * slots * total),
    )(
        device_prompt, resp_len, queries[0, 0], out_grad[0, 0], resp_keys[0, 0], resp_values[0, 0],
        prefix_keys[0], prefix_values[0],
    )
    dquery, dkeys, dvalues, dprefix_keys, dprefix_values = pl.pallas_call(
        publish,
        out_shape=[jax.ShapeDtypeStruct(x.shape, x.dtype) for x in outs],
        in_specs=[anywhere] * len(outs),
        out_specs=[anywhere] * len(outs),
        scratch_shapes=[vmem(x.shape, x.dtype) for x in outs] + [dma((len(outs),))] * 2,
        compiler_params=pltpu.CompilerParams(vmem_limit_bytes=63 * 2**20),
    )(*outs)
    return dquery[None, None], dkeys[None, None], dvalues[None, None], dprefix_keys[None], dprefix_values[None]


def solution(mesh):
    row = P("owner", "resp", None, None)
    return jax.shard_map(
        functools.partial(body, mesh.shape["owner"], mesh.shape["resp"]),
        mesh=mesh,
        in_specs=(row, row, row, row, P("owner", "resp", None), P("owner", "resp", None), P("owner", "resp"), P("owner", "resp")),
        out_specs=(row, row, row, P("owner", "resp", None), P("owner", "resp", None)),
        check_vma=False,
    )
```

time: 188 us -> 49.4 us (0.26)
  waiting for transfers between devices: 74 us -> 0 us
  Pallas kernels: 0 us -> 46.6 us
  starting transfers between devices: 30.8 us -> 0 us
  blocking collectives: 30.3 us -> 0 us
  matrix products: 15.1 us -> 0 us
  between operations: 16 us -> 1.93 us
  local copies, waits for them, and re-layouts: 12.3 us -> 0 us
  other arithmetic: 9.29 us -> 0 us
    reduce_scatter x1 -> x0, waiting for transfers between devices: 66.8 us -> none  [body(): summed = lax.psum_scatter(placed, 'resp', scatter_dimension=2, tiled=True)]
    pallas_call x0 -> x2, Pallas kernels: none -> 46.6 us  [the longest x1 44.5 us: body(): pl.pallas_call(functools.partial(kernel, n_owner, rows, prefix_len, slots...]
    ppermute x4 -> x0, starting transfers between devices: 30.8 us -> none  [the longest x2 18 us: padded(): lax.ppermute(lax.slice_in_dim(block, block.shape[dim] - width, None, axis...]
    all_gather x1 -> x0, blocking collectives: 30.3 us -> none  [body(): whole_prefix = lax.all_gather(stacked, 'resp', axis=2, tiled=True)]
    dot_general x20 -> x0, matrix products: 11.4 us -> none  [the longest x4 3.22 us: head_grads(): jnp.einsum('grk,rgd->kd', dscores, query_head, preferred_element_type=jnp...]
    ppermute x4 -> x0, waiting for transfers between devices: 7.13 us -> none  [the longest x2 4.54 us: padded(): lax.ppermute(lax.slice_in_dim(block, block.shape[dim] - width, None, axis...]
    unnamed x55 -> x0, local copies, waits for them, and re-layouts: 7 us -> none
    sub x4 -> x0, matrix products: 3.68 us -> none  [head_grads(): exp_terms = jnp.exp(scores - row_top)]
  transfers between devices with their start and end apart: 5 -> 0, of which waited for: 4 -> 0; matrix products, arithmetic and copies ran while one was open for 5% -> 0% of each run, Pallas kernels for 0% -> 0%
where the time goes in v3:
time: 49.4 us; the launch traced here: 48.5 us
  Pallas kernels  46.6 us (94%)
  between operations  1.93 us (4%)
    pallas_call x1, Pallas kernels, body(): pl.pallas_call(functools.partial(kernel, n_owner, rows, prefix_len, slots...  44.5 us
    pallas_call x1, Pallas kernels, body(): pl.pallas_call(publish, out_shape=[jax.ShapeDtypeStruct(x.shape, x.dtype)...  2.1 us

profile of v3, /device:TPU:1, one launch (start us, length us, event | category | flops | bytes accessed | tf_op | source)
XLA Modules:
  0.0 48.5 jit_solution(17007173397906647162)
XLA Ops:
  1.9 44.5 %shard_map.119 = (bf16[128,2560]{1,0:T(8,128)(2,1)}, bf16[128,512]{1,0:T(8,128)(2,1)}, bf16[128,512]{1,0:T(8,128)(2,1)}, f32[16,512]{1,0:T(8,128)}, f32[16,512]{1,0:T(8,128)}) custom-call(s32[1,1]{1,0:T(1,128)S(6)} %copy.13.prompt_ref, s32[1,1]{1,0:T(1,128)S(6)} %copy.14.len_ref, bf16[128,2560]{1,0:T(8,128)(2,1)} %bitcast.11, bf16[128,2560]{1,0:T(8,128)(2,1)} %bitcast.12, ...), custom_call_target="tpu_custom_call" | custom-call | flops 1258291200 | bytes 4194304 | tf_op jit(solution)/shard_map/pallas_call | solution.py:429
  46.4 2.1 %shard_map.120 = (bf16[128,2560]{1,0:T(8,128)(2,1)}, bf16[128,512]{1,0:T(8,128)(2,1)}, bf16[128,512]{1,0:T(8,128)(2,1)}, f32[16,512]{1,0:T(8,128)}, f32[16,512]{1,0:T(8,128)}) custom-call(bf16[128,2560]{1,0:T(8,128)(2,1)} %get-tuple-element.15.refs_0_, bf16[128,512]{1,0:T(8,128)(2,1)} %get-tuple-element.16.refs_1_, ...), custom_call_target="tpu_custom_call" | custom-call | tf_op jit(solution)/shard_map/pallas_call | solution.py:477

commit v4 on v3

v4 whole, which is shorter than its diff:
```python
import functools
import math

import jax
import jax.numpy as jnp
from jax import lax
from jax.experimental import pallas as pl
from jax.experimental.pallas import tpu as pltpu
from jax.sharding import PartitionSpec as P

HQ = 20
HK = 4
DH = 128
GROUP = HQ // HK
MESH = pl.DeviceIdType.MESH
F32 = jnp.float32
BF16 = jnp.bfloat16


def dot(a, b, dims):
    return lax.dot_general(a, b, (dims, ((), ())), preferred_element_type=F32)


SLOTS = 4
NY = 8
STEPS = (-1, 3, 1, -3, 4, 0, -2, 2)
KINDS = ((0, 2, 1), (2, 2, -1), (4, 1, None), (5, 3, 0))
PARTS = 2
BANDS = 4
EARLY = 2
PER_PART = HK // PARTS


def slot_weights(tile):
    return [jnp.maximum(1.0 - jnp.abs(tile - s), 0.0) for s in range(SLOTS)]


def kernel(
    n_owner, rows, prefix_len, slots,
    prompt_ref, len_ref, q_hbm, g_hbm, rk_hbm, rv_hbm, pk_hbm, pv_hbm,
    dq_hbm, drk_hbm, drv_hbm, sums_in,
    q_all, g_all, resp_all, near, tiles, stage, kv_all, grad_out, grad_in,
    sums_out, nothing, dq_all, dr_all,
    masked, resp_scores, resp_dprobs, dscores_all,
    store_sem, load_sem, own_sem, near_send, near_recv, tile_send, tile_recv,
    gather_send, gather_recv, grad_send, grad_recv, sums_send, sums_recv,
):
    o = lax.axis_index("owner")
    r = lax.axis_index("resp")
    pairs = n_owner // 2
    k = o // 2
    c = lax.rem(o, 2)
    xl = r // NY
    y = lax.rem(r, NY)
    me = 2 * c + xl
    others = ((1 - c, xl), (c, 1 - xl), (1 - c, 1 - xl))
    prompts = (pk_hbm, pv_hbm)
    has_below = k > 0
    has_above = k < pairs - 1
    side = 2 * c - 1
    next_in = (k + side >= 0) & (k + side < pairs)
    other_in = (k - side >= 0) & (k - side < pairs)
    pair_next = lax.rem(k + side + pairs, pairs)
    pair_other = lax.rem(k - side + pairs, pairs)
    pair_below = lax.rem(k + pairs - 1, pairs)
    pair_above = lax.rem(k + 1, pairs)

    y_of = {step: lax.rem(y + (step + NY), NY) for step in (-2, -1, 0, 1, 2)}
    y_of["far"] = lax.rem(y + (4 * c + NY - 2), NY)

    def device(core, x, step):
        return (2 * k + core, x * NY + y_of[step])

    def column(owner, step):
        return (owner, xl * NY + y_of[step])

    def remote(src, dst, send, recv, target):
        return pltpu.make_async_remote_copy(
            src_ref=src, dst_ref=dst, send_sem=send, recv_sem=recv, device_id=target, device_id_type=MESH
        )

    loads = [
        pltpu.make_async_copy(rk_hbm, resp_all.at[0], load_sem.at[0]),
        pltpu.make_async_copy(rv_hbm, resp_all.at[1], load_sem.at[1]),
        pltpu.make_async_copy(q_hbm, q_all, load_sem.at[2]),
        pltpu.make_async_copy(g_hbm, g_all, load_sem.at[3]),
    ]
    barrier = pltpu.get_barrier_semaphore()

    def signal(target):
        pl.semaphore_signal(barrier, inc=1, device_id=target, device_id_type=MESH)

    for step in (2, -2, 0, 1, -1):
        for spot in range(4):
            if step == 0:
                if spot < 3:
                    signal(device(*others[spot], 0))
            else:
                signal(device(spot // 2, spot % 2, step))

    @pl.when(next_in)
    def _():
        for step in (2, -2, 0):
            for kv in range(2):
                signal(column(2 * pair_next + kv, step))

    @pl.when(other_in)
    def _():
        for step in (2, -2, 0):
            signal(column(2 * pair_other + c, step))

    tiles[0, me] = jnp.full((1, DH), (prompt_ref[0, 0] - (2 * k - 1)).astype(F32))

    blanks = [pltpu.make_async_copy(nothing, sums_in.at[where, 1], store_sem.at[4 + where]) for where in range(3)]

    @pl.when(k == 0)
    def _():
        for where in range(3):
            near[where, 0] = jnp.zeros_like(near[where, 0])

    @pl.when(k == pairs - 1)
    def _():
        for where in range(3):
            near[where, 3] = jnp.zeros_like(near[where, 3])

    @pl.when(jnp.logical_not(next_in))
    def _():
        nothing[...] = jnp.zeros_like(nothing)
        for copy in blanks:
            copy.start()

    own_copies = [pltpu.make_async_copy(prompts[kv], near.at[0, 1 + c], own_sem.at[0]) for kv in range(2)]
    for kv in range(2):
        pl.when(c == kv)(own_copies[kv].start)

    for copy in loads:
        copy.start()
    pl.semaphore_wait(barrier, 19 + 6 * next_in.astype(jnp.int32) + 3 * other_in.astype(jnp.int32))

    def near_copy(where, kind, kv):
        step = {1: 2, 2: -2, 0: 0}[where]
        pair, slot = ((k, 1 + c), (pair_next, 3 - 3 * c))[kind]
        return remote(
            prompts[kv], near.at[where, slot], near_send.at[where, kind, kv], near_recv.at[where, slot],
            column(2 * pair + kv, step),
        )

    def each_near(action):
        @pl.when(next_in)
        def _():
            for where in (1, 2, 0):
                for kv in range(2):
                    getattr(near_copy(where, 1, kv), action)()

        for where in (1, 2):
            for kv in range(2):
                getattr(near_copy(where, 0, kv), action)()
        for kv in range(2):
            pl.when(c != kv)(getattr(near_copy(0, 0, kv), action))

    def tile_copy(core, x, step, kind):
        spot = 2 * core + x
        return remote(
            tiles.at[0, me], tiles.at[kind, me], tile_send.at[kind, spot], tile_recv.at[kind, me], device(core, x, step),
        )

    tile_copies = [
        tile_copy(spot // 2, spot % 2, step, kind) for kind, step in ((1, -1), (2, 1), (3, "far")) for spot in range(4)
    ] + [tile_copy(core, x, 0, 0) for core, x in others]

    def each(copies, action):
        for copy in copies:
            getattr(copy, action)()

    each_near("start")
    each(tile_copies, "start")

    def arrived(ref, sem):
        remote(ref, ref, near_send.at[0, 0, 0], sem, device(0, 0, 1)).wait_recv()

    length = len_ref[0, 0]
    key_index = lax.broadcasted_iota(jnp.int32, (slots, slots), 0)
    row_index = lax.broadcasted_iota(jnp.int32, (slots, slots), 1)
    hidden = jnp.where((key_index <= row_index) & (key_index < length), 0.0, -1e30)
    hidden = jnp.concatenate([hidden] * GROUP, axis=1)
    valid = jnp.where(key_index < length, 1.0, 0.0).astype(BF16)
    scale = 1.0 / math.sqrt(DH)
    exp_scale = scale * math.log2(math.e)

    def columns(ref, first):
        return ref[:, pl.ds(pl.multiple_of(first, DH), DH)]

    def head_queries(h):
        return jnp.concatenate([columns(q_all, (h * GROUP + g) * DH) for g in range(GROUP)], axis=0)

    def prepare(h, carry):
        grads = jnp.concatenate([columns(g_all, (h * GROUP + g) * DH) * valid for g in range(GROUP)], axis=0)
        masked[h] = grads
        resp_scores[h] = dot(columns(resp_all.at[0], h * DH), head_queries(h), ((1,), (1,))) + hidden
        resp_dprobs[h] = dot(columns(resp_all.at[1], h * DH), grads, ((1,), (1,)))
        return carry

    for copy in loads:
        copy.wait()
    lax.fori_loop(0, EARLY, prepare, 0)

    for kind in (1, 2, 3):
        for spot in range(4):
            arrived(tiles.at[kind, spot], tile_recv.at[kind, spot])
    for core, x in others:
        arrived(tiles.at[0, 2 * core + x], tile_recv.at[0, 2 * core + x])

    def near_arrived(where, slot):
        arrived(near.at[where, slot], near_recv.at[where, slot])

    for where in (1, 2):
        near_arrived(where, 1)
        near_arrived(where, 2)
    near_arrived(0, 2 - c)
    for condition, slot in ((has_below, 0), (has_above, 3)):

        @pl.when(condition)
        def _(slot=slot):
            for where in range(3):
                near_arrived(where, slot)

    for kv in range(2):
        pl.when(c == kv)(own_copies[kv].wait)

    weights = [[slot_weights(tiles[kind, spot]) for spot in range(4)] for kind in range(4)]
    weights[0] = [slot_weights(tiles[0, 2 * core + x]) for core, x in others] + [slot_weights(tiles[0, me])]

    def gather_copy(part, spot, kind):
        first, count, _ = KINDS[kind]
        heads = pl.ds(part * PER_PART, PER_PART)
        blocks = pl.ds(first, count)
        if kind == 3:
            target = device(*others[spot], 0)
        else:
            target = device(spot // 2, spot % 2, (-1, 1, 2 if spot < 2 else -2)[kind])
        return remote(
            stage.at[heads, spot, blocks], kv_all.at[heads, c, xl, blocks],
            gather_send.at[part, spot, kind], gather_recv.at[part, me, kind], target,
        )

    gather_copies = []
    for part in range(PARTS):
        for kind in range(4):
            first = KINDS[kind][0]
            for spot in range(4):
                low = [jnp.broadcast_to(w, (rows, DH)).astype(BF16) for w in weights[(2, 1, 3, 0)[kind]][spot]]
                for j, where in enumerate(((1, 2), (2, 1), (1,) if spot < 2 else (2,), (0, 1, 2))[kind]):
                    for h in range(part * PER_PART, (part + 1) * PER_PART):
                        lanes = slice(h * DH, (h + 1) * DH)
                        picked = sum(low[s] * near[where, s, :, lanes] for s in range(SLOTS))
                        if kind == 3 and spot == 3:
                            kv_all[h, c, xl, first + j] = picked
                        else:
                            stage[h, spot, first + j] = picked
                if not (kind == 3 and spot == 3):
                    copy = gather_copy(part, spot, kind)
                    copy.start()
                    gather_copies.append(copy)

    lax.fori_loop(EARLY, HK, prepare, 0)

    def gather_arrived(part):
        heads = pl.ds(part * PER_PART, PER_PART)
        for kind, (first, count, _) in enumerate(KINDS):
            for core, x in others if kind == 3 else ((0, 0), (0, 1), (1, 0), (1, 1)):
                arrived(kv_all.at[heads, core, x, pl.ds(first, count)], gather_recv.at[part, 2 * core + x, kind])

    def grad_copies(h):
        copies = []
        for kind, (first, count, step) in enumerate(KINDS):
            blocks = pl.ds(first, count)
            for core, x in others if kind == 3 else ((0, 0), (0, 1), (1, 0), (1, 1)):
                copies.append(remote(
                    grad_out.at[h, core, x, blocks], grad_in.at[h, me, blocks],
                    grad_send.at[h, 2 * core + x, kind], grad_recv.at[h, me, kind],
                    device(core, x, "far" if kind == 2 else step),
                ))
        return copies

    def each_sum(first, count, action):
        heads = pl.ds(first, count)
        part = 0 if first == 0 else 1

        def act(where, slot, kind, owner):
            copy = remote(
                sums_out.at[where, slot, heads], sums_in.at[where, kind, c, heads],
                sums_send.at[part, where, slot], sums_recv.at[part, where, kind, c],
                column(owner, {1: -2, 2: 2, 0: 0}[where]),
            )
            getattr(copy, action)()

        @pl.when(has_below)
        def _():
            for where in (1, 2, 0):
                act(where, 0, 1, 2 * pair_below + 1)

        @pl.when(has_above)
        def _():
            for where in (1, 2, 0):
                act(where, 3, 1, 2 * pair_above)

        for where in (1, 2):
            act(where, 1, 0, 2 * k)
            act(where, 2, 0, 2 * k + 1)
        act(0, 2 - c, 0, 2 * k + 1 - c)

    def combine(h):
        for kind, (first, count, _) in enumerate(KINDS):
            for core, x in others if kind == 3 else ((0, 0), (0, 1), (1, 0), (1, 1)):
                spot = 2 * core + x
                arrived(grad_in.at[h, spot, pl.ds(first, count)], grad_recv.at[h, spot, kind])

        def piece(block, kind, spot):
            if kind == 0:
                if spot == 3:
                    return grad_out[h, c, xl, block]
                core, x = others[spot]
                return grad_in[h, 2 * core + x, block]
            return grad_in[h, spot, block]

        below = [(6, 0, s) for s in range(4)] + [(0, 2, s) for s in range(4)] + [(3, 1, s) for s in range(4)] + [(4, 3, 0), (4, 3, 1)]
        above = [(7, 0, s) for s in range(4)] + [(1, 2, s) for s in range(4)] + [(2, 1, s) for s in range(4)] + [(4, 3, 2), (4, 3, 3)]
        here = [(5, 0, s) for s in range(4)]
        for where, terms in enumerate((here, below, above)):
            totals = [None] * SLOTS
            for block, kind, spot in terms:
                value = piece(block, kind, spot).astype(F32)
                for s in range(SLOTS):
                    term = weights[kind][spot][s] * value
                    totals[s] = term if totals[s] is None else totals[s] + term
            for s in range(SLOTS):
                sums_out[where, s, h] = totals[s].astype(BF16)

    def attend(h):
        keys = kv_all[h, 0].reshape(prefix_len, DH)
        values = kv_all[h, 1].reshape(prefix_len, DH)
        queries = head_queries(h)
        grads = masked[h]
        scores = jnp.concatenate([dot(keys, queries, ((1,), (1,))), resp_scores[h]], axis=0)
        top = jnp.max(scores, axis=0, keepdims=True)
        terms = jnp.exp2((scores - top) * exp_scale)
        probs = terms * (1.0 / jnp.sum(terms, axis=0, keepdims=True))
        probs_low = probs.astype(BF16)
        dprobs = jnp.concatenate([dot(values, grads, ((1,), (1,))), resp_dprobs[h]], axis=0)
        delta = jnp.sum(probs * dprobs, axis=0, keepdims=True)
        dscores = (probs * (dprobs - delta)).astype(BF16)
        dscores_all[h] = dscores
        dkeys = dot(dscores, queries, ((1,), (0,))) * scale
        dvalues = dot(probs_low, grads, ((1,), (0,)))
        for kv, value in enumerate((dkeys, dvalues)):
            grad_out[h, kv] = value[:prefix_len].astype(BF16).reshape(2, NY, rows, DH)
            dr_all[kv, :, pl.ds(pl.multiple_of(h * DH, DH), DH)] = value[prefix_len:].astype(BF16)
        each(grad_copies(h), "start")

    def query_grads(h, carry):
        keys = jnp.concatenate([kv_all[h, 0].reshape(prefix_len, DH), columns(resp_all.at[0], h * DH)], axis=0)
        keys_t = keys.astype(F32).T.astype(BF16)
        dquery_t = dot(keys_t, dscores_all[h], ((1,), (0,))) * scale
        for g in range(GROUP):
            dquery = dquery_t[:, g * slots:(g + 1) * slots].T.astype(BF16)
            dq_all[:, pl.ds(pl.multiple_of((h * GROUP + g) * DH, DH), DH)] = dquery
        return carry

    def head(h, carry):
        for part in range(PARTS):
            pl.when(h == part * PER_PART)(functools.partial(gather_arrived, part))
        attend(h)
        return carry

    def collect(h, carry):
        combine(h)
        return carry

    lax.fori_loop(0, HK, head, 0)
    stores = [
        pltpu.make_async_copy(held, ref, store_sem.at[i])
        for i, (held, ref) in enumerate((
            (dr_all.at[0], drk_hbm), (dr_all.at[1], drv_hbm), (dq_all, dq_hbm), (sums_out.at[0, 1 + c], sums_in.at[0, 0, c]),
        ))
    ]
    lax.fori_loop(0, HK - 1, collect, 0)
    each_sum(0, HK - 1, "start")
    lax.fori_loop(0, EARLY, query_grads, 0)
    combine(HK - 1)
    each_sum(HK - 1, 1, "start")
    lax.fori_loop(EARLY, HK, query_grads, 0)
    for copy in stores:
        copy.start()
    each_near("wait_send")
    each(tile_copies, "wait_send")
    each(gather_copies, "wait_send")

    def drain(h, carry):
        each(grad_copies(h), "wait_send")
        return carry

    lax.fori_loop(0, HK, drain, 0)

    for part, heads in enumerate((pl.ds(0, HK - 1), pl.ds(HK - 1, 1))):

        def sum_arrived(where, kind, kv):
            arrived(sums_in.at[where, kind, kv, heads], sums_recv.at[part, where, kind, kv])

        sum_arrived(0, 0, 1 - c)
        for where in (1, 2):
            for kv in range(2):
                sum_arrived(where, 0, kv)

        @pl.when(next_in)
        def _():
            for where in range(3):
                for kv in range(2):
                    sum_arrived(where, 1, kv)

    each_sum(0, HK - 1, "wait_send")
    each_sum(HK - 1, 1, "wait_send")
    for copy in stores:
        copy.wait()

    @pl.when(jnp.logical_not(next_in))
    def _():
        for copy in blanks:
            copy.wait()


def publish(
    dq_ref, drk_ref, drv_ref, sums_ref, dq_out, drk_out, drv_out, dpk_out, dpv_out,
    dq, drk, drv, sums, dpk, dpv, in_sem, out_sem,
):
    loads, stores = [], []

    def move(source, held, target):
        sem = len(loads)
        loads.append(pltpu.make_async_copy(source, held, in_sem.at[sem]))
        stores.append(pltpu.make_async_copy(held, target, out_sem.at[sem]))

    sums_load = pltpu.make_async_copy(sums_ref, sums, in_sem.at[BANDS + 2])
    band = dq_ref.shape[0] // BANDS
    for first in range(0, BANDS * band, band):
        span = pl.ds(first, band)
        move(dq_ref.at[span], dq.at[span], dq_out.at[span])
    move(drk_ref, drk, drk_out)
    move(drv_ref, drv, drv_out)
    for copy in loads:
        copy.start()
    sums_load.start()
    for load, store in zip(loads, stores):
        load.wait()
        store.start()
    sums_load.wait()
    for kv, (held, target) in enumerate(((dpk, dpk_out), (dpv, dpv_out))):
        for h in range(HK):
            held[:, h * DH:(h + 1) * DH] = sum(
                sums[where, kind, kv, h].astype(F32) for where in range(3) for kind in range(2)
            )
        copy = pltpu.make_async_copy(held, target, out_sem.at[BANDS + 2 + kv])
        copy.start()
        stores.append(copy)
    for copy in stores:
        copy.wait()


def body(n_owner, n_resp, queries, resp_keys, resp_values, out_grad, prefix_keys, prefix_values, device_prompt, resp_len):
    slots = queries.shape[2]
    rows = prefix_keys.shape[1]
    prefix_len = rows * n_resp
    total = prefix_len + slots
    anywhere = pl.BlockSpec(memory_space=pl.ANY)
    scalar = pl.BlockSpec(memory_space=pltpu.SMEM)
    dma = pltpu.SemaphoreType.DMA
    vmem = pltpu.VMEM
    width = HK * DH
    flops = 2 * 5 * HQ * slots * total * DH
    outs = pl.pallas_call(
        functools.partial(kernel, n_owner, rows, prefix_len, slots),
        out_shape=(
            jax.ShapeDtypeStruct((slots, HQ * DH), BF16),
            jax.ShapeDtypeStruct((slots, width), BF16),
            jax.ShapeDtypeStruct((slots, width), BF16),
            jax.ShapeDtypeStruct((3, 2, 2, HK, rows, DH), BF16),
        ),
        in_specs=[scalar] * 2 + [anywhere] * 6,
        out_specs=(anywhere,) * 4,
        scratch_shapes=[
            vmem((slots, HQ * DH), BF16),
            vmem((slots, HQ * DH), BF16),
            vmem((2, slots, width), BF16),
            vmem((3, SLOTS, rows, width), BF16),
            vmem((4, 4, 1, DH), F32),
            vmem((HK, 4, NY, rows, DH), BF16),
            vmem((HK, 2, 2, NY, rows, DH), BF16),
            vmem((HK, 2, 2, NY, rows, DH), BF16),
            vmem((HK, 4, NY, rows, DH), BF16),
            vmem((3, SLOTS, HK, rows, DH), BF16),
            vmem((2, HK, rows, DH), BF16),
            vmem((slots, HQ * DH), BF16),
            vmem((2, slots, width), BF16),
            vmem((HK, GROUP * slots, DH), BF16),
            vmem((HK, slots, GROUP * slots), F32),
            vmem((HK, slots, GROUP * slots), F32),
            vmem((HK, total, GROUP * slots), BF16),
            dma((7,)),
            dma((4,)),
            dma((1,)),
            dma((3, 2, 2)),
            dma((3, SLOTS)),
            dma((4, 4)),
            dma((4, 4)),
            dma((PARTS, 4, 4)),
            dma((PARTS, 4, 4)),
            dma((HK, 4, 4)),
            dma((HK, 4, 4)),
            dma((2, 3, SLOTS)),
            dma((2, 3, 2, 2)),
        ],
        compiler_params=pltpu.CompilerParams(
            collective_id=0, has_side_effects=True, vmem_limit_bytes=63 * 2**20
        ),
        cost_estimate=pl.CostEstimate(flops=flops, bytes_accessed=4 * 2**20, transcendentals=HQ * slots * total),
    )(
        device_prompt, resp_len, queries[0, 0], out_grad[0, 0], resp_keys[0, 0], resp_values[0, 0],
        prefix_keys[0], prefix_values[0],
    )
    results = [jax.ShapeDtypeStruct(x.shape, x.dtype) for x in outs[:3]] + [jax.ShapeDtypeStruct((rows, width), F32)] * 2
    dquery, dkeys, dvalues, dprefix_keys, dprefix_values = pl.pallas_call(
        publish,
        out_shape=results,
        in_specs=[anywhere] * len(outs),
        out_specs=[anywhere] * len(results),
        scratch_shapes=[vmem(x.shape, x.dtype) for x in (*outs, *results[3:])] + [dma((BANDS + 4,))] * 2,
        compiler_params=pltpu.CompilerParams(vmem_limit_bytes=63 * 2**20),
    )(*outs)
    return dquery[None, None], dkeys[None, None], dvalues[None, None], dprefix_keys[None], dprefix_values[None]


def solution(mesh):
    row = P("owner", "resp", None, None)
    return jax.shard_map(
        functools.partial(body, mesh.shape["owner"], mesh.shape["resp"]),
        mesh=mesh,
        in_specs=(row, row, row, row, P("owner", "resp", None), P("owner", "resp", None), P("owner", "resp"), P("owner", "resp")),
        out_specs=(row, row, row, P("owner", "resp", None), P("owner", "resp", None)),
        check_vma=False,
    )
```

time: 49.4 us -> 45.5 us (0.921)
  Pallas kernels: 46.6 us -> 42.8 us
    pallas_call x1, Pallas kernels: 44.5 us -> 40.7 us  [body(): pl.pallas_call(functools.partial(kernel, n_owner, rows, prefix_len, slots...]
where the time goes in v4:
time: 45.5 us; the launch traced here: 44.7 us
  Pallas kernels  42.8 us (94%)
  between operations  1.93 us (4%)
    pallas_call x1, Pallas kernels, body(): pl.pallas_call(functools.partial(kernel, n_owner, rows, prefix_len, slots...  40.7 us
    pallas_call x1, Pallas kernels, body(): pl.pallas_call(publish, out_shape=results, in_specs=[anywhere] * len(outs...  2.11 us

profile of v4, /device:TPU:1, one launch (start us, length us, event | category | flops | bytes accessed | tf_op | source)
XLA Modules:
  0.0 44.7 jit_solution(655050501262950805)
XLA Ops:
  1.9 40.7 %shard_map.119 = (bf16[128,2560]{1,0:T(8,128)(2,1)}, bf16[128,512]{1,0:T(8,128)(2,1)}, bf16[128,512]{1,0:T(8,128)(2,1)}, bf16[3,2,2,4,16,128]{5,4,3,2,1,0:T(8,128)(2,1)}) custom-call(s32[1,1]{1,0:T(1,128)S(6)} %copy.13.prompt_ref, s32[1,1]{1,0:T(1,128)S(6)} %copy.14.len_ref, bf16[128,2560]{1,0:T(8,128)(2,1)} %bitcast.11, bf16[128,2560]{1,0:T(8,128)(2,1)} %bitcast.12, ...), custom_call_target="tpu_custom_call" | custom-call | flops 1258291200 | bytes 4194304 | tf_op jit(solution)/shard_map/pallas_call | solution.py:479
  42.6 2.1 %shard_map.120 = (bf16[128,2560]{1,0:T(8,128)(2,1)}, bf16[128,512]{1,0:T(8,128)(2,1)}, bf16[128,512]{1,0:T(8,128)(2,1)}, f32[16,512]{1,0:T(8,128)}, f32[16,512]{1,0:T(8,128)}) custom-call(bf16[128,2560]{1,0:T(8,128)(2,1)} %get-tuple-element.14.dq_ref, bf16[128,512]{1,0:T(8,128)(2,1)} %get-tuple-element.15.drk_ref, ...), custom_call_target="tpu_custom_call" | custom-call | tf_op jit(solution)/shard_map/pallas_call | solution.py:530
